TPU v7x, 512 devices: a whole 4x4x16 slice. The times are simulated.
512 devices in a mesh: ao: 64 (over y, z), grp: 8 (over x, core).
Axes of the slice: x: 4, y: 4, z: 16, core: 2. Of those that a mesh axis runs over, the one named last changes fastest.
Arguments:
- three_center: bfloat16 [8, 512, 28672], P(None, 'grp', 'ao'), may hold values from -6 to 6
- occ_density: bfloat16 [8, 64, 64, 448], P('grp', 'ao'), may hold values from -0.25 to 0.25
- virt_density: bfloat16 [8, 64, 64, 448], P('grp', 'ao'), may hold values from -0.25 to 0.25
- tensor_mask: int32 [8, 64, 7], replicated, may hold values 0 or 1
- occ_mask: int32 [8, 64, 7], replicated, may hold values 0 or 1
- virt_mask: int32 [8, 64, 7], replicated, may hold values 0 or 1
- block_sizes: int32 [8, 64], replicated, may hold values from 32 to 64
Outputs:
- polarizability: float32 [8, 8], P('grp')
All inputs are finite; a program needn't handle non-finite values.
Results may differ from a plain program's by a relative error of at most 0.0043.
Values may be sent and summed in bfloat16 or wider, within the bound.
A program may use at most 64 MiB of HBM per device.

v0:
```python
import math

import jax
import jax.numpy as jnp
from jax import lax
from jax.sharding import PartitionSpec as P

stencil_steps = ((0, 0, 0), (-1, 0, 0), (1, 0, 0), (0, -1, 0), (0, 1, 0), (0, 0, -1), (0, 0, 1))
reverse_step = (0, 2, 1, 4, 3, 6, 5)


def passed_along(x, axis, by):
    count = lax.axis_size(axis)
    pairs = [(i, i + by) for i in range(count) if 0 <= i + by < count]
    return lax.ppermute(x, axis, pairs)


def reach_table():
    found = []
    for first_step in stencil_steps:
        for second_step in stencil_steps:
            total = (
                first_step[0] + second_step[0],
                first_step[1] + second_step[1],
                first_step[2] + second_step[2],
            )
            if total not in found:
                found.append(total)
    return found


def offset_between(first_step, second_step, factor):
    return (
        first_step[0] + factor * second_step[0],
        first_step[1] + factor * second_step[1],
        first_step[2] + factor * second_step[2],
    )


def neighbour_row(ao_index, grp_index, line_size, axis_size, group_size):
    depth_at = ao_index // line_size
    along_at = ao_index % line_size
    entries = []
    for first_step in stencil_steps:
        first_to = grp_index + first_step[0]
        second_to = depth_at + first_step[1]
        third_to = along_at + first_step[2]
        inside = (
            (first_to >= 0)
            & (first_to < group_size)
            & (second_to >= 0)
            & (second_to < axis_size // line_size)
            & (third_to >= 0)
            & (third_to < line_size)
        )
        entries.append(
            jnp.where(
                inside,
                first_to * axis_size + second_to * line_size + third_to,
                axis_size * group_size,
            )
        )
    return jnp.stack(entries)


def masked_square(density, mask_table, block_sizes, nearby, block_index, block_width, block_count):
    sizes_ext = jnp.concatenate([block_sizes.reshape(-1), jnp.zeros((1,), jnp.int32)])
    compare = jnp.arange(block_count + 1, dtype=jnp.int32)[None, :] == nearby[:, None]
    beside = jnp.sum(jnp.where(compare, sizes_ext[None, :], 0), axis=1)
    mask_row = lax.dynamic_index_in_dim(mask_table.reshape(-1, 7), block_index, 0, keepdims=False)
    valid = nearby < block_count
    offsets = jnp.arange(block_width, dtype=jnp.int32)
    column_keep = (
        (offsets[None, :] < beside[:, None]) & (mask_row[:, None] > 0) & valid[:, None]
    ).reshape(1, 7 * block_width)
    row_keep = (offsets < beside[0])[:, None]
    square = density.reshape(block_width, 7 * block_width)
    return jnp.where(row_keep & column_keep, square, jnp.zeros_like(square))


def pick_columns(half_tensor, which, reach, block_width):
    pieces = []
    for target_step in stencil_steps:
        target = reach.index(offset_between(target_step, stencil_steps[which], -1))
        pieces.append(half_tensor[:, :, target * block_width : (target + 1) * block_width])
    return jnp.concatenate(pieces, axis=2)


def fetch_virtual(virt_square, line_size):
    fetched = []
    for distance in (1, -1):
        fetched.append(passed_along(virt_square, "grp", distance))
    for distance in (line_size, -line_size, 1, -1):
        fetched.append(passed_along(virt_square, "ao", distance))
    return fetched


def fetch_terms(terms, line_size):
    fetched = []
    for which, distance in ((1, 1), (2, -1)):
        fetched.append(passed_along(terms[which], "grp", distance))
    for which, distance in ((3, line_size), (4, -line_size), (5, 1), (6, -1)):
        fetched.append(passed_along(terms[which], "ao", distance))
    return fetched


def product_with(tensor_cols, virt_row):
    return jnp.dot(tensor_cols, virt_row, preferred_element_type=jnp.float32)


def mix_term(occ_piece, columns):
    return jnp.einsum("ml,pms->pls", occ_piece, columns, preferred_element_type=jnp.float32)


def body(three_center, occ_density, virt_density, tensor_mask, occ_mask, virt_mask, block_sizes):
    block_width = occ_density.shape[2]
    axis_size = lax.axis_size("ao")
    group_size = lax.axis_size("grp")
    line_size = axis_size // 4
    block_count = axis_size * group_size
    ao_index = lax.axis_index("ao")
    grp_index = lax.axis_index("grp")
    block_index = grp_index * axis_size + ao_index
    nearby = neighbour_row(ao_index, grp_index, line_size, axis_size, group_size)
    reach = reach_table()
    regrouped = lax.all_to_all(three_center, "ao", split_axis=1, concat_axis=2, tiled=True)
    slab_rows = regrouped.shape[0]
    occ_square = masked_square(
        occ_density, occ_mask, block_sizes, nearby, block_index, block_width, block_count
    )
    virt_square = masked_square(
        virt_density, virt_mask, block_sizes, nearby, block_index, block_width, block_count
    )
    mask_row = lax.dynamic_index_in_dim(tensor_mask.reshape(-1, 7), block_index, 0, keepdims=False)
    column_on = (mask_row > 0) & (nearby < block_count)
    column_weight = jnp.repeat(
        column_on.astype(jnp.bfloat16), block_width, total_repeat_length=7 * block_width
    )
    tensor_local = (
        regrouped.reshape(slab_rows * block_width, 7 * block_width) * column_weight[None, :]
    )
    virt_rows = [virt_square] + fetch_virtual(virt_square, line_size)
    slots = [None] * len(reach)
    for which in range(7):
        tensor_cols = tensor_local[:, which * block_width : (which + 1) * block_width]
        product = product_with(tensor_cols, virt_rows[which])
        for other in range(7):
            target = reach.index(offset_between(stencil_steps[which], stencil_steps[other], 1))
            portion = product[:, other * block_width : (other + 1) * block_width]
            slots[target] = portion if slots[target] is None else slots[target] + portion
    half_tensor = (
        jnp.concatenate(slots, axis=1)
        .astype(jnp.bfloat16)
        .reshape(slab_rows, block_width, len(reach) * block_width)
    )
    terms = []
    for which in range(7):
        back_at = reverse_step[which]
        occ_piece = occ_square[:, back_at * block_width : (back_at + 1) * block_width]
        columns = pick_columns(half_tensor, which, reach, block_width)
        terms.append(mix_term(occ_piece, columns))
    received = fetch_terms(terms, line_size)
    mixed_sum = terms[0]
    for entry in received:
        mixed_sum = mixed_sum + entry
    contracted = mixed_sum.astype(jnp.bfloat16)
    partial_value = lax.dot_general(
        contracted.reshape(slab_rows, -1),
        tensor_local.reshape(slab_rows, -1),
        (((1,), (1,)), ((), ())),
        preferred_element_type=jnp.float32,
    )
    partial_value = partial_value / (block_width * math.sqrt(block_count))
    rows_out = slab_rows // group_size
    summed = lax.psum(partial_value, ("ao", "grp"))
    return lax.dynamic_slice_in_dim(summed, grp_index * rows_out, rows_out, 0)


def solution(mesh):
    in_specs = (
        P(None, "grp", "ao"),
        P("grp", "ao", None, None),
        P("grp", "ao", None, None),
        P(),
        P(),
        P(),
        P(),
    )
    out_specs = P("grp", None)
    return jax.shard_map(body, mesh=mesh, in_specs=in_specs, out_specs=out_specs, check_vma=False)
```

profile of v0, /device:TPU:1, one launch (start us, length us, event | category | flops | bytes accessed | tf_op | source)
XLA Modules:
  0.0 262.6 jit_solution(14220934229854311915)
XLA Ops:
  0.0 2.1 copy.73
  2.1 19.3 %all-to-all-start = ((bf16[8,64,448]{2,0,1:T(8,128)(2,1)}), bf16[8,64,448]{2,0,1:T(8,128)(2,1)S(1)}, u32[]{:S(2)}, u32[]{:S(2)}) async-start(bf16[8,64,448]{2,0,1:T(8,128)(2,1)} %copy.73), calls=%async_computation | async-start | bytes 1048576 | tf_op jit(solution)/shard_map/all_to_all | solution.py:126
  28.3 4.0 %collective-permute-start.4 = (bf16[64,448]{0,1:T(8,128)(2,1)S(1)}, bf16[64,448]{0,1:T(8,128)(2,1)S(1)}, u32[]{:S(2)}, u32[]{:S(2)}) collective-permute-start(bf16[64,448]{0,1:T(8,128)(2,1)S(1)} %get-tuple-element.39), channel_id=1, source_target_pairs={{0,8},{8,16},{16,24},{24,32},{32,40},{40,48},{48,56},{56,64},{64,7... | collective-permute-start | bytes 172040 | tf_op jit(solution)/shard_map/ppermute | solution.py:15
  33.6 4.5 %collective-permute-start.2 = (bf16[64,448]{0,1:T(8,128)(2,1)S(1)}, bf16[64,448]{0,1:T(8,128)(2,1)S(1)}, u32[]{:S(2)}, u32[]{:S(2)}) collective-permute-start(bf16[64,448]{0,1:T(8,128)(2,1)S(1)} %get-tuple-element.39), channel_id=1, source_target_pairs={{0,128},{8,136},{16,144},{24,152},{32,160},{40,168},{48,176},{56,1... | collective-permute-start | bytes 172040 | tf_op jit(solution)/shard_map/ppermute | solution.py:15
  38.1 3.7 %collective-permute-start.1 = (bf16[64,448]{0,1:T(8,128)(2,1)S(1)}, bf16[64,448]{0,1:T(8,128)(2,1)}, u32[]{:S(2)}, u32[]{:S(2)}) collective-permute-start(bf16[64,448]{0,1:T(8,128)(2,1)S(1)} %get-tuple-element.39), channel_id=1, source_target_pairs={{1,0},{2,1},{3,2},{4,3},{5,4},{6,5},{7,6},{9,8},{10,9},{11,10},{12... | collective-permute-start | bytes 172040 | tf_op jit(solution)/shard_map/ppermute | solution.py:15
  42.6 4.3 %and_select_fusion.2 = bf16[448]{0:T(512)(128)(2,1)S(1)} fusion(s32[512]{0:T(512)S(1)} %add_bitcast_fusion, bf16[]{:T(256)} %bitcast.11, bf16[]{:T(256)} %bitcast.12, bf16[]{:T(256)} %bitcast.13, bf16[]{:T(256)} %bitcast.14, bf16[]{:T(256)} %bitcast.15, bf16[]{:T(256)} %bitcast.16, bf16[]{:T(256)} %bitcast.17), kind=kLoop, calls=%fused_computation.112 | loop fusion | flops 8960 | bytes 2702 | tf_op jit(solution)/shard_map/jit(_take)/select_n | solution.py:136
  46.9 3.8 %all-to-all-done = bf16[8,64,448]{2,0,1:T(8,128)(2,1)S(1)} async-done(((bf16[8,64,448]{2,0,1:T(8,128)(2,1)}), bf16[8,64,448]{2,0,1:T(8,128)(2,1)S(1)}, u32[]{:S(2)}, u32[]{:S(2)}) %all-to-all-start) | async-done | bytes 458784 | tf_op jit(solution)/shard_map/all_to_all | solution.py:126
  51.3 7.2 %collective-permute-start = (bf16[64,448]{0,1:T(8,128)(2,1)S(1)}, bf16[64,448]{0,1:T(8,128)(2,1)S(1)}, u32[]{:S(2)}, u32[]{:S(2)}) collective-permute-start(bf16[64,448]{0,1:T(8,128)(2,1)S(1)} %get-tuple-element.39), channel_id=1, source_target_pairs={{0,1},{1,2},{2,3},{3,4},{4,5},{5,6},{6,7},{8,9},{9,10},{10,11},{11... | collective-permute-start | bytes 172040 | tf_op jit(solution)/shard_map/ppermute | solution.py:15
  70.4 1.6 copy.151
  75.2 1.6 copy.153
  80.0 1.6 copy.148
  86.3 2.0 concatenate.120
  88.3 2.3 convolution_bitcast_fusion.4
  90.7 2.0 concatenate.132
  92.7 2.3 convolution_bitcast_fusion
  96.3 2.0 concatenate.124
  98.4 2.3 convolution_bitcast_fusion.3
  108.2 4.7 %collective-permute-start.8 = (f32[8,64,448]{2,1,0:T(8,128)}, f32[8,64,448]{2,1,0:T(8,128)}, u32[]{:S(2)}, u32[]{:S(2)}) collective-permute-start(f32[8,64,448]{2,1,0:T(8,128)} %convolution_bitcast_fusion.3), channel_id=1, source_target_pairs={{0,128},{8,136},{16,144},{24,152},{32,160},{40,168},{48,176},{56,1... | collective-permute-start | bytes 2752520 | tf_op jit(solution)/shard_map/ppermute | solution.py:15
  120.0 4.7 %collective-permute-start.6 = (f32[8,64,448]{2,1,0:T(8,128)}, f32[8,64,448]{2,1,0:T(8,128)}, u32[]{:S(2)}, u32[]{:S(2)}) collective-permute-start(f32[8,64,448]{2,1,0:T(8,128)} %convolution_bitcast_fusion.5), channel_id=1, source_target_pairs={{0,1},{1,2},{2,3},{3,4},{4,5},{5,6},{6,7},{8,9},{9,10},{10,11},{11... | collective-permute-start | bytes 2752520 | tf_op jit(solution)/shard_map/ppermute | solution.py:15
  124.6 4.6 %collective-permute-start.10 = (f32[8,64,448]{2,1,0:T(8,128)}, f32[8,64,448]{2,1,0:T(8,128)}, u32[]{:S(2)}, u32[]{:S(2)}) collective-permute-start(f32[8,64,448]{2,1,0:T(8,128)} %convolution_bitcast_fusion.1), channel_id=1, source_target_pairs={{0,8},{8,16},{16,24},{24,32},{32,40},{40,48},{48,56},{56,64},{64,7... | collective-permute-start | bytes 2752520 | tf_op jit(solution)/shard_map/ppermute | solution.py:15
  130.5 1.9 collective-permute-start.7
  132.9 22.8 %collective-permute-done.8 = f32[8,64,448]{2,1,0:T(8,128)} collective-permute-done((f32[8,64,448]{2,1,0:T(8,128)}, f32[8,64,448]{2,1,0:T(8,128)}, u32[]{:S(2)}, u32[]{:S(2)}) %collective-permute-start.8) | collective-permute-done | bytes 917536 | tf_op jit(solution)/shard_map/ppermute | solution.py:15
  155.7 3.2 %fusion.6 = bf16[8,64,448]{2,1,0:T(8,128)(2,1)S(1)} fusion(f32[8,64,448]{2,1,0:T(8,128)} %collective-permute-done.11, f32[8,64,448]{2,1,0:T(8,128)} %collective-permute-done.10, f32[8,64,448]{2,1,0:T(8,128)} %collective-permute-done.9, f32[8,64,448]{2,1,0:T(8,128)} %collective-permute-done.8, f32[8,64,448]{2,1,0:T(8,128)} %collective-permute-done.7, ...), kind=kOutput, calls=%fused_computation.13 | convolution fusion | flops 30965760 | bytes 6504448 | tf_op jit(solution)/shard_map/ml,pms->pls/dot_general | solution.py:112
  159.5 102.6 %psum.7 = f32[8,8]{1,0:T(8,128)S(1)} all-reduce(f32[8,8]{1,0:T(8,128)S(1)} %fusion.7), channel_id=1, replica_groups=mesh['ao'=64,'grp'=8] {'ao','grp'}, use_global_device_ids=true, to_apply=%region_1.2 | all-reduce | flops 64 | bytes 512 | tf_op jit(solution)/shard_map/psum | solution.py:175
  (133 shorter events, 50.6 us)
Async XLA Ops:
  2.1 48.6 %all-to-all-start = ((bf16[8,64,448]{2,0,1:T(8,128)(2,1)}), bf16[8,64,448]{2,0,1:T(8,128)(2,1)S(1)}, u32[]{:S(2)}, u32[]{:S(2)}) async-start(bf16[8,64,448]{2,0,1:T(8,128)(2,1)} %copy.73), calls=%async_computation | async-start | bytes 1048576 | tf_op jit(solution)/shard_map/all_to_all | solution.py:126
  21.4 0.8 copy-start.18
  27.0 24.3 %collective-permute-start.5 = (bf16[64,448]{0,1:T(8,128)(2,1)S(1)}, bf16[64,448]{0,1:T(8,128)(2,1)S(1)}, u32[]{:S(2)}, u32[]{:S(2)}) collective-permute-start(bf16[64,448]{0,1:T(8,128)(2,1)S(1)} %get-tuple-element.39), channel_id=1, source_target_pairs={{8,0},{16,8},{24,16},{32,24},{40,32},{48,40},{56,48},{64,56},{72,6... | collective-permute-start | bytes 172040 | tf_op jit(solution)/shard_map/ppermute | solution.py:15
  28.3 32.3 %collective-permute-start.4 = (bf16[64,448]{0,1:T(8,128)(2,1)S(1)}, bf16[64,448]{0,1:T(8,128)(2,1)S(1)}, u32[]{:S(2)}, u32[]{:S(2)}) collective-permute-start(bf16[64,448]{0,1:T(8,128)(2,1)S(1)} %get-tuple-element.39), channel_id=1, source_target_pairs={{0,8},{8,16},{16,24},{24,32},{32,40},{40,48},{48,56},{56,64},{64,7... | collective-permute-start | bytes 172040 | tf_op jit(solution)/shard_map/ppermute | solution.py:15
  32.3 28.7 %collective-permute-start.3 = (bf16[64,448]{0,1:T(8,128)(2,1)S(1)}, bf16[64,448]{0,1:T(8,128)(2,1)S(1)}, u32[]{:S(2)}, u32[]{:S(2)}) collective-permute-start(bf16[64,448]{0,1:T(8,128)(2,1)S(1)} %get-tuple-element.39), channel_id=1, source_target_pairs={{128,0},{136,8},{144,16},{152,24},{160,32},{168,40},{176,48},{184,... | collective-permute-start | bytes 172040 | tf_op jit(solution)/shard_map/ppermute | solution.py:15
  33.6 25.1 %collective-permute-start.2 = (bf16[64,448]{0,1:T(8,128)(2,1)S(1)}, bf16[64,448]{0,1:T(8,128)(2,1)S(1)}, u32[]{:S(2)}, u32[]{:S(2)}) collective-permute-start(bf16[64,448]{0,1:T(8,128)(2,1)S(1)} %get-tuple-element.39), channel_id=1, source_target_pairs={{0,128},{8,136},{16,144},{24,152},{32,160},{40,168},{48,176},{56,1... | collective-permute-start | bytes 172040 | tf_op jit(solution)/shard_map/ppermute | solution.py:15
  38.1 24.4 %collective-permute-start.1 = (bf16[64,448]{0,1:T(8,128)(2,1)S(1)}, bf16[64,448]{0,1:T(8,128)(2,1)}, u32[]{:S(2)}, u32[]{:S(2)}) collective-permute-start(bf16[64,448]{0,1:T(8,128)(2,1)S(1)} %get-tuple-element.39), channel_id=1, source_target_pairs={{1,0},{2,1},{3,2},{4,3},{5,4},{6,5},{7,6},{9,8},{10,9},{11,10},{12... | collective-permute-start | bytes 172040 | tf_op jit(solution)/shard_map/ppermute | solution.py:15
  51.3 9.0 %collective-permute-start = (bf16[64,448]{0,1:T(8,128)(2,1)S(1)}, bf16[64,448]{0,1:T(8,128)(2,1)S(1)}, u32[]{:S(2)}, u32[]{:S(2)}) collective-permute-start(bf16[64,448]{0,1:T(8,128)(2,1)S(1)} %get-tuple-element.39), channel_id=1, source_target_pairs={{0,1},{1,2},{2,3},{3,4},{4,5},{5,6},{6,7},{8,9},{9,10},{10,11},{11... | collective-permute-start | bytes 172040 | tf_op jit(solution)/shard_map/ppermute | solution.py:15
  65.3 0.9 copy-start.14
  95.0 35.5 %collective-permute-start.11 = (f32[8,64,448]{2,1,0:T(8,128)}, f32[8,64,448]{2,1,0:T(8,128)}, u32[]{:S(2)}, u32[]{:S(2)}) collective-permute-start(f32[8,64,448]{2,1,0:T(8,128)} %convolution_bitcast_fusion), channel_id=1, source_target_pairs={{8,0},{16,8},{24,16},{32,24},{40,32},{48,40},{56,48},{64,56},{72,6... | collective-permute-start | bytes 2752520 | tf_op jit(solution)/shard_map/ppermute | solution.py:15
  107.3 5.7 %copy-start.7 = (bf16[512,64]{1,0:T(8,128)(2,1)S(1)}, bf16[512,64]{1,0:T(8,128)(2,1)}, u32[]{:S(2)}) copy-start(bf16[512,64]{1,0:T(8,128)(2,1)} %copy.148) | copy-start | bytes 196612
  107.4 5.6 %copy-start.6 = (bf16[512,64]{1,0:T(8,128)(2,1)S(1)}, bf16[512,64]{1,0:T(8,128)(2,1)}, u32[]{:S(2)}) copy-start(bf16[512,64]{1,0:T(8,128)(2,1)} %copy.147) | copy-start | bytes 196612
  108.2 47.4 %collective-permute-start.8 = (f32[8,64,448]{2,1,0:T(8,128)}, f32[8,64,448]{2,1,0:T(8,128)}, u32[]{:S(2)}, u32[]{:S(2)}) collective-permute-start(f32[8,64,448]{2,1,0:T(8,128)} %convolution_bitcast_fusion.3), channel_id=1, source_target_pairs={{0,128},{8,136},{16,144},{24,152},{32,160},{40,168},{48,176},{56,1... | collective-permute-start | bytes 2752520 | tf_op jit(solution)/shard_map/ppermute | solution.py:15
  113.0 0.9 copy-start.3
  113.0 1.0 copy-start.4
  114.0 1.3 copy-start.2
  114.0 1.3 copy-start.5
  115.3 0.9 copy-start.8
  118.7 13.8 %copy-start = (bf16[512,64]{1,0:T(8,128)(2,1)S(1)}, bf16[512,64]{1,0:T(8,128)(2,1)}, u32[]{:S(2)}) copy-start(bf16[512,64]{1,0:T(8,128)(2,1)} %copy.144) | copy-start | bytes 196612
  118.7 13.8 %copy-start.1 = (bf16[512,64]{1,0:T(8,128)(2,1)S(1)}, bf16[512,64]{1,0:T(8,128)(2,1)}, u32[]{:S(2)}) copy-start(bf16[512,64]{1,0:T(8,128)(2,1)} %copy.143) | copy-start | bytes 196612
  120.0 35.7 %collective-permute-start.6 = (f32[8,64,448]{2,1,0:T(8,128)}, f32[8,64,448]{2,1,0:T(8,128)}, u32[]{:S(2)}, u32[]{:S(2)}) collective-permute-start(f32[8,64,448]{2,1,0:T(8,128)} %convolution_bitcast_fusion.5), channel_id=1, source_target_pairs={{0,1},{1,2},{2,3},{3,4},{4,5},{5,6},{6,7},{8,9},{9,10},{10,11},{11... | collective-permute-start | bytes 2752520 | tf_op jit(solution)/shard_map/ppermute | solution.py:15
  124.6 31.1 %collective-permute-start.10 = (f32[8,64,448]{2,1,0:T(8,128)}, f32[8,64,448]{2,1,0:T(8,128)}, u32[]{:S(2)}, u32[]{:S(2)}) collective-permute-start(f32[8,64,448]{2,1,0:T(8,128)} %convolution_bitcast_fusion.1), channel_id=1, source_target_pairs={{0,8},{8,16},{16,24},{24,32},{32,40},{40,48},{48,56},{56,64},{64,7... | collective-permute-start | bytes 2752520 | tf_op jit(solution)/shard_map/ppermute | solution.py:15
  129.2 26.5 %collective-permute-start.9 = (f32[8,64,448]{2,1,0:T(8,128)}, f32[8,64,448]{2,1,0:T(8,128)}, u32[]{:S(2)}, u32[]{:S(2)}) collective-permute-start(f32[8,64,448]{2,1,0:T(8,128)} %convolution_bitcast_fusion.2), channel_id=1, source_target_pairs={{128,0},{136,8},{144,16},{152,24},{160,32},{168,40},{176,48},{184,... | collective-permute-start | bytes 2752520 | tf_op jit(solution)/shard_map/ppermute | solution.py:15
  130.5 25.2 %collective-permute-start.7 = (f32[8,64,448]{2,1,0:T(8,128)}, f32[8,64,448]{2,1,0:T(8,128)}, u32[]{:S(2)}, u32[]{:S(2)}) collective-permute-start(f32[8,64,448]{2,1,0:T(8,128)} %convolution_bitcast_fusion.4), channel_id=1, source_target_pairs={{1,0},{2,1},{3,2},{4,3},{5,4},{6,5},{7,6},{9,8},{10,9},{11,10},{12... | collective-permute-start | bytes 2752520 | tf_op jit(solution)/shard_map/ppermute | solution.py:15
  (14 other events, 11.2 us)
where the time goes:
time: 265 us; the launch traced here: 263 us
  blocking collectives  103 us (39%)
  starting transfers between devices  59.7 us (23%)
  local copies, waits for them, and re-layouts  46.2 us (17%)
  waiting for transfers between devices  27.7 us (10%)
  matrix products  17.6 us (7%)
  other arithmetic  8.08 us (3%)
    psum x1, blocking collectives, body(): summed = lax.psum(partial_value, ('ao', 'grp'))  103 us
    ppermute x12, starting transfers between devices, passed_along(): return lax.ppermute(x, axis, pairs)  40.4 us
    ppermute x12, waiting for transfers between devices, passed_along(): return lax.ppermute(x, axis, pairs)  23.9 us
    concatenate x26, local copies, waits for them, and re-layouts, body(): jnp.concatenate(slots, axis=1).astype(jnp.bfloat16)  22.2 us
    all_to_all x1, starting transfers between devices, body(): lax.all_to_all(three_center, 'ao', split_axis=1, concat_axis=2, tiled=True)  19.3 us
    dot_general x7, matrix products, mix_term(): jnp.einsum('ml,pms->pls', occ_piece, columns, preferred_element_type=jnp....  14 us
    unnamed x53, local copies, waits for them, and re-layouts  11.8 us
    concatenate x6, local copies, waits for them, and re-layouts, pick_columns(): return jnp.concatenate(pieces, axis=2)  8.2 us
  transfers between devices with their start and end apart: 13, of which 3 were waited for; matrix products, arithmetic and copies ran while one was open for 9% of the time, Pallas kernels for 0%

commit v1 on v0

v1 whole, which is shorter than its diff:
```python
import functools
import math

import jax
import jax.numpy as jnp
from jax import lax
from jax.experimental import pallas as pl
from jax.experimental.pallas import tpu as pltpu
from jax.sharding import PartitionSpec as P

MESH = pl.DeviceIdType.MESH
BF16 = jnp.bfloat16
F32 = jnp.float32
STEPS = ((0, 0, 0), (-1, 0, 0), (1, 0, 0), (0, -1, 0), (0, 1, 0), (0, 0, -1), (0, 0, 1))


def second_step(i, j, k):
    want = tuple(STEPS[i][x] + STEPS[j][x] - STEPS[k][x] for x in range(3))
    return STEPS.index(want) if want in STEPS else None


def kernel(
    dims,
    t_ref,
    occ_ref,
    virt_ref,
    tm_ref,
    om_ref,
    vm_ref,
    sz_ref,
    out_ref,
    snd,
    arr,
    tn,
    vn,
    vs,
    xs,
    oexp,
    psend,
    r1,
    r2,
    r3,
    a2a_send,
    a2a_recv,
    ex_send,
    ex_recv,
    v_send,
    v_recv,
    r_send,
    r_recv,
):
    groups, rows, line, slab, bs = dims
    n_ao = rows * line
    width = 7 * bs
    g = lax.axis_index("grp")
    a = lax.axis_index("ao")
    y = a // line
    z = a % line

    def moved(step, sign):
        gg = (g + sign * step[0] + groups) % groups
        yy = (y + sign * step[1] + rows) % rows
        zz = (z + sign * step[2] + line) % line
        return gg, yy * line + zz

    def exists(first, second=(0, 0, 0)):
        gg = g + first[0] + second[0]
        yy = y + first[1] + second[1]
        zz = z + first[2] + second[2]
        inside = (gg >= 0) & (gg < groups) & (yy >= 0) & (yy < rows) & (zz >= 0) & (zz < line)
        return inside.astype(jnp.int32)

    barrier = pltpu.get_barrier_semaphore()

    def greet_ao(d, carry):
        pl.semaphore_signal(
            barrier, inc=1, device_id={"ao": (a + d) % n_ao, "grp": g}, device_id_type=MESH
        )
        return carry

    lax.fori_loop(1, n_ao, greet_ao, 0)

    def greet_grp(d, carry):
        pl.semaphore_signal(
            barrier, inc=1, device_id={"ao": a, "grp": (g + d) % groups}, device_id_type=MESH
        )
        return carry

    lax.fori_loop(1, groups, greet_grp, 0)

    part = n_ao // 2
    n_rows = part * slab
    to = lax.broadcasted_iota(jnp.int32, (n_rows, n_rows), 0)
    frm = lax.broadcasted_iota(jnp.int32, (n_rows, n_rows), 1)
    perm = jnp.where(frm == (to % slab) * part + to // slab, 1.0, 0.0).astype(BF16)
    for half in range(2):
        rows_in = t_ref[:, half * part : (half + 1) * part, :].reshape(n_rows, width)
        moved_rows = jnp.dot(perm, rows_in, preferred_element_type=F32)
        snd[half * part : (half + 1) * part] = moved_rows.reshape(part, slab, width).astype(BF16)

    lane = lax.broadcasted_iota(jnp.int32, (1, width), 1)
    lane_block = lane // bs
    lane_in = lane % bs
    row_at = lax.broadcasted_iota(jnp.int32, (bs, 1), 0)
    size_here = sz_ref[g, a]

    def masked(density, mask_ref):
        bound = jnp.zeros((1, width), jnp.int32)
        for k in range(7):
            gk, ak = moved(STEPS[k], 1)
            value = sz_ref[gk, ak] * mask_ref[k, g, a] * exists(STEPS[k])
            bound = bound + jnp.where(lane_block == k, value, 0)
        keep_col = jnp.where(lane_in < bound, 1.0, 0.0)
        keep_row = jnp.where(row_at < size_here, 1.0, 0.0)
        return (density.astype(F32) * (keep_row * keep_col)).astype(BF16)

    vn[0] = masked(virt_ref[...], vm_ref)

    pl.semaphore_wait(barrier, n_ao - 1 + groups - 1)

    def to_neighbour(ref, k, send, recv):
        gk, ak = moved(STEPS[k], -1)
        return pltpu.make_async_remote_copy(
            src_ref=ref.at[0],
            dst_ref=ref.at[k],
            send_sem=send.at[k - 1],
            recv_sem=recv.at[k - 1],
            device_id={"ao": ak, "grp": gk},
            device_id_type=MESH,
        )

    v_copies = [to_neighbour(vn, k, v_send, v_recv) for k in range(1, 7)]
    for copy in v_copies:
        copy.start()

    def give(d, carry):
        turn = d // rows
        far = line // 2 - (turn + 1) // 2
        z_to = (z + far * (2 * (turn % 2) - 1) + line) % line
        y_to = (y + rows - 1 - d % rows) % rows
        target = y_to * line + z_to
        pltpu.make_async_remote_copy(
            src_ref=snd.at[target],
            dst_ref=arr.at[a],
            send_sem=a2a_send,
            recv_sem=a2a_recv,
            device_id={"ao": target, "grp": g},
            device_id_type=MESH,
        ).start()
        return carry

    lax.fori_loop(0, n_ao - 1, give, 0)
    arr[a] = snd[a]

    occ = masked(occ_ref[...], om_ref)
    spread_rows = jnp.where(
        lax.broadcasted_iota(jnp.int32, (bs * slab, bs), 0) // slab
        == lax.broadcasted_iota(jnp.int32, (bs * slab, bs), 1),
        1.0,
        0.0,
    ).astype(BF16)
    spread_cols = jnp.where(
        lax.broadcasted_iota(jnp.int32, (bs, bs * slab), 1) // slab
        == lax.broadcasted_iota(jnp.int32, (bs, bs * slab), 0),
        1.0,
        0.0,
    ).astype(BF16)
    for i in range(7):
        tall = jnp.dot(spread_rows, occ[:, i * bs : (i + 1) * bs], preferred_element_type=F32)
        oexp[i] = jnp.dot(tall.astype(BF16), spread_cols, preferred_element_type=F32)

    col_on = []
    for i in range(7):
        gi, ai = moved(STEPS[i], 1)
        on = jnp.zeros((1, width), jnp.int32)
        for j in range(7):
            value = tm_ref[j, gi, ai] * exists(STEPS[i], STEPS[j])
            on = on + jnp.where(lane_block == j, value, 0)
        col_on.append(on.astype(F32))
    for k in range(7):
        if k:
            v_copies[k - 1].wait_recv()
        row_on = (tm_ref[k, g, a] * exists(STEPS[k])).astype(F32)
        v_row = vn[k].astype(F32) * row_on
        for i in range(7):
            pieces = []
            for j in range(7):
                k2 = second_step(i, j, k)
                if k2 is None:
                    pieces.append(jnp.zeros((bs, bs), F32))
                else:
                    pieces.append(v_row[:, k2 * bs : (k2 + 1) * bs])
            placed = jnp.concatenate(pieces, axis=1) * col_on[i]
            vs[i, k * bs : (k + 1) * bs, :] = placed.astype(BF16)

    pltpu.make_async_copy(arr.at[pl.ds(0, n_ao - 1)], arr.at[pl.ds(0, n_ao - 1)], a2a_recv).wait()
    tn[0] = arr[...].astype(F32).reshape(bs * slab, width).astype(BF16)
    t_copies = [to_neighbour(tn, k, ex_send, ex_recv) for k in range(1, 7)]
    for copy in t_copies:
        copy.start()

    own = tn[0]
    for i in range(7):
        xs[i] = jnp.dot(own, vs[i], preferred_element_type=F32).astype(BF16)
    total = jnp.zeros((slab, bs * slab), F32)
    for i in range(7):
        if i:
            t_copies[i - 1].wait_recv()
        pairs = lax.dot_general(
            xs[i], tn[i], (((1,), (1,)), ((), ())), preferred_element_type=F32
        )
        weighted = pairs * oexp[i]
        total = total + jnp.sum(weighted.reshape(bs, slab, bs * slab), axis=0)

    part_sum = total[:, 0:128]
    for at in range(1, bs * slab // 128):
        part_sum = part_sum + total[:, at * 128 : (at + 1) * 128]
    shift = 64
    while shift >= slab:
        part_sum = part_sum + pltpu.roll(part_sum, shift, 1)
        shift //= 2

    for p in range(slab):
        psend[p] = part_sum[p : p + 1, :]

    def all_slots(buf, count):
        acc = buf[0]
        for at in range(1, count):
            acc = acc + buf[at]
        return acc

    def wait_bytes(buf, count, sem):
        ref = buf.at[pl.ds(0, count - 1)]
        pltpu.make_async_copy(ref, ref, sem).wait()

    def to_grp(d, carry):
        gg = (g + d) % groups
        pltpu.make_async_remote_copy(
            src_ref=psend.at[gg],
            dst_ref=r1.at[g],
            send_sem=r_send.at[0],
            recv_sem=r_recv.at[0],
            device_id={"ao": a, "grp": gg},
            device_id_type=MESH,
        ).start()
        return carry

    lax.fori_loop(1, groups, to_grp, 0)
    r1[g] = psend[g]
    wait_bytes(r1, groups, r_recv.at[0])
    r2[y] = all_slots(r1, groups)

    def to_rows(d, carry):
        yy = (y + d) % rows
        pltpu.make_async_remote_copy(
            src_ref=r2.at[y],
            dst_ref=r2.at[y],
            send_sem=r_send.at[1],
            recv_sem=r_recv.at[1],
            device_id={"ao": yy * line + z, "grp": g},
            device_id_type=MESH,
        ).start()
        return carry

    lax.fori_loop(1, rows, to_rows, 0)
    wait_bytes(r2, rows, r_recv.at[1])
    r3[z] = all_slots(r2, rows)

    def to_line(d, carry):
        zz = (z + d) % line
        pltpu.make_async_remote_copy(
            src_ref=r3.at[z],
            dst_ref=r3.at[z],
            send_sem=r_send.at[2],
            recv_sem=r_recv.at[2],
            device_id={"ao": y * line + zz, "grp": g},
            device_id_type=MESH,
        ).start()
        return carry

    lax.fori_loop(1, line, to_line, 0)
    wait_bytes(r3, line, r_recv.at[2])
    out_ref[...] = all_slots(r3, line) * (1.0 / (bs * math.sqrt(groups * n_ao)))

    for copy in v_copies + t_copies:
        copy.wait_send()
    wait_bytes(snd, n_ao, a2a_send)
    wait_bytes(r1, groups, r_send.at[0])
    wait_bytes(r2, rows, r_send.at[1])
    wait_bytes(r3, line, r_send.at[2])


def body(three_center, occ_density, virt_density, tensor_mask, occ_mask, virt_mask, block_sizes):
    groups = lax.axis_size("grp")
    n_ao = lax.axis_size("ao")
    rows = 4
    line = n_ao // rows
    slab = three_center.shape[0]
    bs = occ_density.shape[2]
    width = 7 * bs
    dims = (groups, rows, line, slab, bs)
    in_vmem = pl.BlockSpec(memory_space=pltpu.VMEM)
    in_smem = pl.BlockSpec(memory_space=pltpu.SMEM)
    result = pl.pallas_call(
        functools.partial(kernel, dims),
        out_shape=jax.ShapeDtypeStruct((1, 128), F32),
        in_specs=[in_vmem] * 3 + [in_smem] * 4,
        out_specs=in_vmem,
        scratch_shapes=[
            pltpu.VMEM((n_ao, slab, width), BF16),
            pltpu.VMEM((n_ao, slab, width), BF16),
            pltpu.VMEM((7, bs * slab, width), BF16),
            pltpu.VMEM((7, bs, width), BF16),
            pltpu.VMEM((7, width, width), BF16),
            pltpu.VMEM((7, bs * slab, width), BF16),
            pltpu.VMEM((7, bs * slab, bs * slab), F32),
            pltpu.VMEM((slab, 1, 128), F32),
            pltpu.VMEM((groups, 1, 128), F32),
            pltpu.VMEM((rows, 1, 128), F32),
            pltpu.VMEM((line, 1, 128), F32),
            pltpu.SemaphoreType.DMA,
            pltpu.SemaphoreType.DMA,
            pltpu.SemaphoreType.DMA((6,)),
            pltpu.SemaphoreType.DMA((6,)),
            pltpu.SemaphoreType.DMA((6,)),
            pltpu.SemaphoreType.DMA((6,)),
            pltpu.SemaphoreType.DMA((3,)),
            pltpu.SemaphoreType.DMA((3,)),
        ],
        compiler_params=pltpu.CompilerParams(
            collective_id=0, has_side_effects=True, vmem_limit_bytes=48 * 1024 * 1024
        ),
    )(
        three_center,
        occ_density.reshape(bs, width),
        virt_density.reshape(bs, width),
        jnp.transpose(tensor_mask, (2, 0, 1)),
        jnp.transpose(occ_mask, (2, 0, 1)),
        jnp.transpose(virt_mask, (2, 0, 1)),
        block_sizes,
    )
    return result[:, :slab]


def solution(mesh):
    in_specs = (
        P(None, "grp", "ao"),
        P("grp", "ao", None, None),
        P("grp", "ao", None, None),
        P(),
        P(),
        P(),
        P(),
    )
    return jax.shard_map(
        body, mesh=mesh, in_specs=in_specs, out_specs=P("grp", None), check_vma=False
    )
```

time: 265 us -> 79 us (0.30)
  blocking collectives: 103 us -> 0 us
  Pallas kernels: 0 us -> 72.3 us
  starting transfers between devices: 59.7 us -> 0 us
  local copies, waits for them, and re-layouts: 46.2 us -> 6.16 us
  waiting for transfers between devices: 27.7 us -> 0 us
  matrix products: 17.6 us -> 0 us
  other arithmetic: 8.08 us -> 0 us
    psum x1 -> x0, blocking collectives: 103 us -> none  [body(): summed = lax.psum(partial_value, ('ao', 'grp'))]
    pallas_call x0 -> x1, Pallas kernels: none -> 72.3 us  [body(): pl.pallas_call(functools.partial(kernel, dims), out_shape=jax.ShapeDtypeS...]
    ppermute x12 -> x0, starting transfers between devices: 40.4 us -> none  [passed_along(): return lax.ppermute(x, axis, pairs)]
    concatenate x32 -> x0, local copies, waits for them, and re-layouts: 30.4 us -> none  [the longest x26 22.2 us: body(): jnp.concatenate(slots, axis=1).astype(jnp.bfloat16)]
    ppermute x12 -> x0, waiting for transfers between devices: 23.9 us -> none  [passed_along(): return lax.ppermute(x, axis, pairs)]
    all_to_all x1 -> x0, starting transfers between devices: 19.3 us -> none  [body(): lax.all_to_all(three_center, 'ao', split_axis=1, concat_axis=2, tiled=True)]
    dot_general x15 -> x0, matrix products: 17.6 us -> none  [the longest x7 14 us: mix_term(): jnp.einsum('ml,pms->pls', occ_piece, columns, preferred_element_type=jnp....]
    unnamed x53 -> x15, local copies, waits for them, and re-layouts: 11.8 us -> 6.16 us
  transfers between devices with their start and end apart: 13 -> 0, of which waited for: 3 -> 0; matrix products, arithmetic and copies ran while one was open for 9% -> 0% of each run, Pallas kernels for 0% -> 0%
where the time goes in v1:
time: 79 us; the launch traced here: 78.5 us
  Pallas kernels  72.3 us (92%)
  local copies, waits for them, and re-layouts  6.16 us (8%)
    pallas_call x1, Pallas kernels, body(): pl.pallas_call(functools.partial(kernel, dims), out_shape=jax.ShapeDtypeS...  72.3 us
    unnamed x15, local copies, waits for them, and re-layouts  6.16 us

profile of v1, /device:TPU:1, one launch (start us, length us, event | category | flops | bytes accessed | tf_op | source)
XLA Modules:
  0.0 78.5 jit_solution(7347080528837985876)
XLA Ops:
  0.0 0.0 copy-start.6
  0.0 0.7 copy-done.6
  0.7 0.0 copy-start
  0.7 1.0 %copy-done = bf16[8,64,448]{2,1,0:T(8,128)(2,1)S(1)} copy-done((bf16[8,64,448]{2,1,0:T(8,128)(2,1)S(1)}, bf16[8,64,448]{2,1,0:T(8,128)(2,1)}, u32[]{:S(2)}) %copy-start) | copy-done | bytes 458776
  1.7 0.0 copy-start.1
  1.7 0.8 %copy-done.1 = bf16[1,1,64,448]{3,2,1,0:T(8,128)(2,1)S(1)} copy-done((bf16[1,1,64,448]{3,2,1,0:T(8,128)(2,1)S(1)}, bf16[1,1,64,448]{3,2,1,0:T(8,128)(2,1)}, u32[]{:S(2)}) %copy-start.1) | copy-done | bytes 57368
  2.6 0.0 copy-start.2
  2.6 0.8 %copy-done.2 = bf16[1,1,64,448]{3,2,1,0:T(8,128)(2,1)S(1)} copy-done((bf16[1,1,64,448]{3,2,1,0:T(8,128)(2,1)S(1)}, bf16[1,1,64,448]{3,2,1,0:T(8,128)(2,1)}, u32[]{:S(2)}) %copy-start.2) | copy-done | bytes 57368
  3.4 0.0 copy-start.3
  3.4 0.7 copy-done.3
  4.2 0.0 copy-start.4
  4.2 0.7 copy-done.4
  4.9 0.0 copy-start.5
  4.9 0.7 copy-done.5
  5.7 72.3 %shard_map.73 = f32[1,128]{1,0:T(1,128)S(1)} custom-call(bf16[8,64,448]{2,1,0:T(8,128)(2,1)S(1)} %copy-done, bf16[64,448]{1,0:T(8,128)(2,1)S(1)} %bitcast.6, bf16[64,448]{1,0:T(8,128)(2,1)S(1)} %bitcast.7, s32[7,8,64]{2,1,0:T(8,128)S(1)} %bitcast.8, s32[7,8,64]{2,1,0:T(8,128)S(1)} %bitcast.9, s32[7,8,64]{2,1,0:T(8,128)S(1)} %bitcast.10, s32[8,64]{1,0:T(8,128)S(1)} %copy-done.6), custom_call_target="tpu_custom_call" | custom-call | tf_op jit(solution)/shard_map/pallas_call | solution.py:304
  78.0 0.5 copy.9
Async XLA Ops:
  0.0 0.7 copy-start.6
  0.7 1.0 %copy-start = (bf16[8,64,448]{2,1,0:T(8,128)(2,1)S(1)}, bf16[8,64,448]{2,1,0:T(8,128)(2,1)}, u32[]{:S(2)}) copy-start(bf16[8,64,448]{2,1,0:T(8,128)(2,1)} %t_ref.1) | copy-start | bytes 1376260
  1.7 0.8 %copy-start.1 = (bf16[1,1,64,448]{3,2,1,0:T(8,128)(2,1)S(1)}, bf16[1,1,64,448]{3,2,1,0:T(8,128)(2,1)}, u32[]{:S(2)}) copy-start(bf16[1,1,64,448]{3,2,1,0:T(8,128)(2,1)} %param.8) | copy-start | bytes 172036
  2.6 0.8 %copy-start.2 = (bf16[1,1,64,448]{3,2,1,0:T(8,128)(2,1)S(1)}, bf16[1,1,64,448]{3,2,1,0:T(8,128)(2,1)}, u32[]{:S(2)}) copy-start(bf16[1,1,64,448]{3,2,1,0:T(8,128)(2,1)} %param.9) | copy-start | bytes 172036
  3.4 0.7 copy-start.3
  4.2 0.7 copy-start.4
  4.9 0.7 copy-start.5

commit v2 on v1

--- a/solution.py
+++ b/solution.py
@@ -21,6 +21,14 @@
 
 def kernel(
     dims,
+    t_hbm,
+    occ_hbm,
+    virt_hbm,
+    tm_hbm,
+    om_hbm,
+    vm_hbm,
+    sz_hbm,
+    out_ref,
     t_ref,
     occ_ref,
     virt_ref,
@@ -28,7 +36,7 @@
     om_ref,
     vm_ref,
     sz_ref,
-    out_ref,
+    load_sem,
     snd,
     arr,
     tn,
@@ -38,7 +46,6 @@
     oexp,
     psend,
     r1,
-    r2,
     r3,
     a2a_send,
     a2a_recv,
@@ -70,6 +77,21 @@
         inside = (gg >= 0) & (gg < groups) & (yy >= 0) & (yy < rows) & (zz >= 0) & (zz < line)
         return inside.astype(jnp.int32)
 
+    loads = []
+    for at, (source, target) in enumerate(
+        (
+            (virt_hbm, virt_ref),
+            (vm_hbm, vm_ref),
+            (sz_hbm, sz_ref),
+            (t_hbm, t_ref),
+            (occ_hbm, occ_ref),
+            (om_hbm, om_ref),
+            (tm_hbm, tm_ref),
+        )
+    ):
+        loads.append(pltpu.make_async_copy(source, target, load_sem.at[at]))
+        loads[-1].start()
+
     barrier = pltpu.get_barrier_semaphore()
 
     def greet_ao(d, carry):
@@ -80,15 +102,19 @@
 
     lax.fori_loop(1, n_ao, greet_ao, 0)
 
-    def greet_grp(d, carry):
+    def greet_sheet(d, carry):
+        gg = (g + 1 + d // rows) % groups
+        yy = (y + d) % rows
         pl.semaphore_signal(
-            barrier, inc=1, device_id={"ao": a, "grp": (g + d) % groups}, device_id_type=MESH
-        )
-        return carry
-
-    lax.fori_loop(1, groups, greet_grp, 0)
+            barrier, inc=1, device_id={"ao": yy * line + z, "grp": gg}, device_id_type=MESH
+        )
+        return carry
+
+    lax.fori_loop(0, (groups - 1) * rows, greet_sheet, 0)
+
 
     part = n_ao // 2
+    loads[3].wait()
     n_rows = part * slab
     to = lax.broadcasted_iota(jnp.int32, (n_rows, n_rows), 0)
     frm = lax.broadcasted_iota(jnp.int32, (n_rows, n_rows), 1)
@@ -102,6 +128,8 @@
     lane_block = lane // bs
     lane_in = lane % bs
     row_at = lax.broadcasted_iota(jnp.int32, (bs, 1), 0)
+    for at in (0, 1, 2):
+        loads[at].wait()
     size_here = sz_ref[g, a]
 
     def masked(density, mask_ref):
@@ -116,7 +144,7 @@
 
     vn[0] = masked(virt_ref[...], vm_ref)
 
-    pl.semaphore_wait(barrier, n_ao - 1 + groups - 1)
+    pl.semaphore_wait(barrier, n_ao - 1 + (groups - 1) * rows)
 
     def to_neighbour(ref, k, send, recv):
         gk, ak = moved(STEPS[k], -1)
@@ -152,6 +180,8 @@
     lax.fori_loop(0, n_ao - 1, give, 0)
     arr[a] = snd[a]
 
+    for at in (4, 5, 6):
+        loads[at].wait()
     occ = masked(occ_ref[...], om_ref)
     spread_rows = jnp.where(
         lax.broadcasted_iota(jnp.int32, (bs * slab, bs), 0) // slab
@@ -233,61 +263,46 @@
         ref = buf.at[pl.ds(0, count - 1)]
         pltpu.make_async_copy(ref, ref, sem).wait()
 
-    def to_grp(d, carry):
-        gg = (g + d) % groups
+    def to_sheet(d, carry):
+        gg = (g + d // rows) % groups
+        yy = (y + d % rows) % rows
         pltpu.make_async_remote_copy(
             src_ref=psend.at[gg],
-            dst_ref=r1.at[g],
+            dst_ref=r1.at[g * rows + y],
             send_sem=r_send.at[0],
             recv_sem=r_recv.at[0],
-            device_id={"ao": a, "grp": gg},
+            device_id={"ao": yy * line + z, "grp": gg},
             device_id_type=MESH,
         ).start()
         return carry
 
-    lax.fori_loop(1, groups, to_grp, 0)
-    r1[g] = psend[g]
-    wait_bytes(r1, groups, r_recv.at[0])
-    r2[y] = all_slots(r1, groups)
-
-    def to_rows(d, carry):
-        yy = (y + d) % rows
-        pltpu.make_async_remote_copy(
-            src_ref=r2.at[y],
-            dst_ref=r2.at[y],
-            send_sem=r_send.at[1],
-            recv_sem=r_recv.at[1],
-            device_id={"ao": yy * line + z, "grp": g},
-            device_id_type=MESH,
-        ).start()
-        return carry
-
-    lax.fori_loop(1, rows, to_rows, 0)
-    wait_bytes(r2, rows, r_recv.at[1])
-    r3[z] = all_slots(r2, rows)
+    lax.fori_loop(1, groups * rows, to_sheet, 0)
+    r1[g * rows + y] = psend[g]
+    wait_bytes(r1, groups * rows, r_recv.at[0])
+    r3[z] = all_slots(r1, groups * rows)
 
     def to_line(d, carry):
         zz = (z + d) % line
         pltpu.make_async_remote_copy(
             src_ref=r3.at[z],
             dst_ref=r3.at[z],
-            send_sem=r_send.at[2],
-            recv_sem=r_recv.at[2],
+            send_sem=r_send.at[1],
+            recv_sem=r_recv.at[1],
             device_id={"ao": y * line + zz, "grp": g},
             device_id_type=MESH,
         ).start()
         return carry
 
     lax.fori_loop(1, line, to_line, 0)
-    wait_bytes(r3, line, r_recv.at[2])
-    out_ref[...] = all_slots(r3, line) * (1.0 / (bs * math.sqrt(groups * n_ao)))
+    wait_bytes(r3, line, r_recv.at[1])
+    scale = 1.0 / (bs * math.sqrt(groups * n_ao))
+    out_ref[...] = (all_slots(r3, line) * scale)[:, :slab]
 
     for copy in v_copies + t_copies:
         copy.wait_send()
     wait_bytes(snd, n_ao, a2a_send)
-    wait_bytes(r1, groups, r_send.at[0])
-    wait_bytes(r2, rows, r_send.at[1])
-    wait_bytes(r3, line, r_send.at[2])
+    wait_bytes(r1, groups * rows, r_send.at[0])
+    wait_bytes(r3, line, r_send.at[1])
 
 
 def body(three_center, occ_density, virt_density, tensor_mask, occ_mask, virt_mask, block_sizes):
@@ -300,13 +315,20 @@
     width = 7 * bs
     dims = (groups, rows, line, slab, bs)
     in_vmem = pl.BlockSpec(memory_space=pltpu.VMEM)
-    in_smem = pl.BlockSpec(memory_space=pltpu.SMEM)
     result = pl.pallas_call(
         functools.partial(kernel, dims),
-        out_shape=jax.ShapeDtypeStruct((1, 128), F32),
-        in_specs=[in_vmem] * 3 + [in_smem] * 4,
+        out_shape=jax.ShapeDtypeStruct((1, slab), F32),
+        in_specs=[pl.BlockSpec(memory_space=pltpu.HBM)] * 7,
         out_specs=in_vmem,
         scratch_shapes=[
+            pltpu.VMEM((slab, n_ao, width), BF16),
+            pltpu.VMEM((bs, width), BF16),
+            pltpu.VMEM((bs, width), BF16),
+            pltpu.SMEM((7, groups, n_ao), jnp.int32),
+            pltpu.SMEM((7, groups, n_ao), jnp.int32),
+            pltpu.SMEM((7, groups, n_ao), jnp.int32),
+            pltpu.SMEM((groups, n_ao), jnp.int32),
+            pltpu.SemaphoreType.DMA((7,)),
             pltpu.VMEM((n_ao, slab, width), BF16),
             pltpu.VMEM((n_ao, slab, width), BF16),
             pltpu.VMEM((7, bs * slab, width), BF16),
@@ -315,8 +337,7 @@
             pltpu.VMEM((7, bs * slab, width), BF16),
             pltpu.VMEM((7, bs * slab, bs * slab), F32),
             pltpu.VMEM((slab, 1, 128), F32),
-            pltpu.VMEM((groups, 1, 128), F32),
-            pltpu.VMEM((rows, 1, 128), F32),
+            pltpu.VMEM((groups * rows, 1, 128), F32),
             pltpu.VMEM((line, 1, 128), F32),
             pltpu.SemaphoreType.DMA,
             pltpu.SemaphoreType.DMA,
@@ -324,11 +345,11 @@
             pltpu.SemaphoreType.DMA((6,)),
             pltpu.SemaphoreType.DMA((6,)),
             pltpu.SemaphoreType.DMA((6,)),
-            pltpu.SemaphoreType.DMA((3,)),
-            pltpu.SemaphoreType.DMA((3,)),
+            pltpu.SemaphoreType.DMA((2,)),
+            pltpu.SemaphoreType.DMA((2,)),
         ],
         compiler_params=pltpu.CompilerParams(
-            collective_id=0, has_side_effects=True, vmem_limit_bytes=48 * 1024 * 1024
+            collective_id=0, has_side_effects=True, vmem_limit_bytes=60 * 1024 * 1024
         ),
     )(
         three_center,
@@ -339,7 +360,7 @@
         jnp.transpose(virt_mask, (2, 0, 1)),
         block_sizes,
     )
-    return result[:, :slab]
+    return result
 
 
 def solution(mesh):

time: 79 us -> 71.5 us (0.905)
  local copies, waits for them, and re-layouts: 6.16 us -> 1.19 us
  Pallas kernels: 72.3 us -> 70.2 us
    unnamed x15 -> x1, local copies, waits for them, and re-layouts: 6.16 us -> 1.19 us
    pallas_call x1, Pallas kernels: 72.3 us -> 70.2 us  [body(): pl.pallas_call(functools.partial(kernel, dims), out_shape=jax.ShapeDtypeS...]
where the time goes in v2:
time: 71.5 us; the launch traced here: 71.4 us
  Pallas kernels  70.2 us (98%)
  local copies, waits for them, and re-layouts  1.19 us (2%)
    pallas_call x1, Pallas kernels, body(): pl.pallas_call(functools.partial(kernel, dims), out_shape=jax.ShapeDtypeS...  70.2 us

profile of v2, /device:TPU:1, one launch (start us, length us, event | category | flops | bytes accessed | tf_op | source)
XLA Modules:
  0.0 71.4 jit_solution(10138424604469171776)
XLA Ops:
  0.0 70.2 %shard_map.73 = f32[1,8]{1,0:T(1,128)} custom-call(bf16[8,64,448]{2,1,0:T(8,128)(2,1)} %t_hbm.1, bf16[64,448]{1,0:T(8,128)(2,1)} %bitcast.5, bf16[64,448]{1,0:T(8,128)(2,1)} %bitcast.6, s32[7,8,64]{2,1,0:T(8,128)} %bitcast.7, s32[7,8,64]{2,1,0:T(8,128)} %bitcast.8, s32[7,8,64]{2,1,0:T(8,128)} %bitcast.9, s32[8,64]{1,0:T(8,128)} %sz_hbm.1), custom_call_target="tpu_custom_call" | custom-call | tf_op jit(solution)/shard_map/pallas_call | solution.py:318
  70.2 1.2 %copy.9 = f32[1,8]{1,0:T(1,128)} copy(f32[1,8]{1,0:T(1,128)} %shard_map.73) | data formatting | bytes 64

commit v3 on v2

v3 whole, which is shorter than its diff:
```python
import functools
import math

import jax
import jax.numpy as jnp
from jax import lax
from jax.experimental import pallas as pl
from jax.experimental.pallas import tpu as pltpu
from jax.sharding import PartitionSpec as P

MESH = pl.DeviceIdType.MESH
BF16 = jnp.bfloat16
F32 = jnp.float32
STEPS = ((0, 0, 0), (-1, 0, 0), (1, 0, 0), (0, -1, 0), (0, 1, 0), (0, 0, -1), (0, 0, 1))
BACK = (0, 2, 1, 4, 3, 6, 5)
PARTS = 4


def second_step(i, j, k):
    want = tuple(STEPS[i][x] + STEPS[j][x] - STEPS[k][x] for x in range(3))
    return STEPS.index(want) if want in STEPS else None


def kernel(
    dims,
    t_hbm,
    occ_hbm,
    virt_hbm,
    tm_hbm,
    om_hbm,
    vm_hbm,
    sz_hbm,
    out_ref,
    t_ref,
    occ_ref,
    virt_ref,
    tm_ref,
    om_ref,
    vm_ref,
    sz_ref,
    load_sem,
    snd,
    arr,
    tn,
    vn,
    pack,
    vs,
    xs,
    oexp,
    psend,
    r1,
    r3,
    a2a_send,
    a2a_recv,
    ex_send,
    ex_recv,
    v_send,
    v_recv,
    p_send,
    p_recv,
    r_send,
    r_recv,
):
    groups, rows, line, slab, bs = dims
    n_ao = rows * line
    width = 7 * bs
    tall = bs * slab
    g = lax.axis_index("grp")
    a = lax.axis_index("ao")
    y = a // line
    z = a % line
    odd = g % 2
    way = 1 - 2 * odd

    def shifted(dg, dy, dz):
        gg = (g + dg + groups) % groups
        yy = (y + dy + rows) % rows
        zz = (z + dz + line) % line
        return gg, yy * line + zz

    def exists(first, second=(0, 0, 0)):
        gg = g + first[0] + second[0]
        yy = y + first[1] + second[1]
        zz = z + first[2] + second[2]
        inside = (gg >= 0) & (gg < groups) & (yy >= 0) & (yy < rows) & (zz >= 0) & (zz < line)
        return inside.astype(jnp.int32)

    barrier = pltpu.get_barrier_semaphore()

    def far_first(d):
        turn = d // rows
        far = line // 2 - (turn + 1) // 2
        z_to = (z + far * (2 * (turn % 2) - 1) + line) % line
        y_to = (y + rows - 1 - d % rows) % rows
        return y_to * line + z_to

    def greet_ao(d, carry):
        pl.semaphore_signal(
            barrier, inc=1, device_id={"ao": far_first(d), "grp": g}, device_id_type=MESH
        )
        return carry

    lax.fori_loop(0, n_ao - 1, greet_ao, 0)

    def greet_sheet(d, carry):
        gg = (g + 1 + d // rows) % groups
        yy = (y + d) % rows
        pl.semaphore_signal(
            barrier, inc=1, device_id={"ao": yy * line + z, "grp": gg}, device_id_type=MESH
        )
        return carry

    lax.fori_loop(0, (groups - 1) * rows, greet_sheet, 0)

    loads = []
    for at, (source, target) in enumerate(
        (
            (t_hbm, t_ref),
            (virt_hbm, virt_ref),
            (vm_hbm, vm_ref),
            (sz_hbm, sz_ref),
            (occ_hbm, occ_ref),
            (om_hbm, om_ref),
            (tm_hbm, tm_ref),
        )
    ):
        loads.append(pltpu.make_async_copy(source, target, load_sem.at[at]))
        loads[-1].start()

    lane = lax.broadcasted_iota(jnp.int32, (1, width), 1)
    lane_block = lane // bs
    lane_in = lane % bs
    row_at = lax.broadcasted_iota(jnp.int32, (bs, 1), 0)

    def masked(density, mask_ref):
        bound = jnp.zeros((1, width), jnp.int32)
        for k in range(7):
            gk, ak = shifted(*STEPS[k])
            value = sz_ref[gk, ak] * mask_ref[k, g, a] * exists(STEPS[k])
            bound = bound + jnp.where(lane_block == k, value, 0)
        keep_col = jnp.where(lane_in < bound, 1.0, 0.0)
        keep_row = jnp.where(row_at < sz_ref[g, a], 1.0, 0.0)
        return (density.astype(F32) * (keep_row * keep_col)).astype(BF16)

    for at in (1, 2, 3):
        loads[at].wait()
    vn[0] = masked(virt_ref[...], vm_ref)

    loads[0].wait()
    part = n_ao // 2
    n_rows = part * slab
    to = lax.broadcasted_iota(jnp.int32, (n_rows, n_rows), 0)
    frm = lax.broadcasted_iota(jnp.int32, (n_rows, n_rows), 1)
    perm = jnp.where(frm == (to % slab) * part + to // slab, 1.0, 0.0).astype(BF16)
    for half in range(2):
        rows_in = t_ref[:, half * part : (half + 1) * part, :].reshape(n_rows, width)
        moved_rows = jnp.dot(perm, rows_in, preferred_element_type=F32)
        snd[half * part : (half + 1) * part] = moved_rows.reshape(part, slab, width).astype(BF16)

    pl.semaphore_wait(barrier, n_ao - 1 + (groups - 1) * rows)

    def v_copy(k):
        gk, ak = shifted(*(-x for x in STEPS[k]))
        return pltpu.make_async_remote_copy(
            src_ref=vn.at[0],
            dst_ref=vn.at[k],
            send_sem=v_send.at[k - 1],
            recv_sem=v_recv.at[k - 1],
            device_id={"ao": ak, "grp": gk},
            device_id_type=MESH,
        )

    v_copies = [v_copy(k) for k in range(1, 7)]
    for copy in v_copies:
        copy.start()

    def give(d, carry):
        target = far_first(d)
        pltpu.make_async_remote_copy(
            src_ref=snd.at[target],
            dst_ref=arr.at[d],
            send_sem=a2a_send,
            recv_sem=a2a_recv.at[d // (n_ao // PARTS)],
            device_id={"ao": target, "grp": g},
            device_id_type=MESH,
        ).start()
        return carry

    first_sends = n_ao // PARTS
    lax.fori_loop(0, first_sends, give, 0)
    arr[n_ao - 1] = snd[a]

    for at in (4, 5, 6):
        loads[at].wait()
    occ = masked(occ_ref[...], om_ref)

    for copy in v_copies:
        copy.wait_recv()

    def towards(parity, axis):
        return (4 if parity == 0 else 3) if axis == 0 else (6 if parity == 0 else 5)

    def others(step):
        return [k for k in range(1, 7) if k != step]

    def block_of(value, k):
        return value[:, k * bs : (k + 1) * bs]

    for parity in range(2):

        @pl.when(odd == parity)
        def _(parity=parity):
            for axis in range(2):
                step = towards(parity, axis)
                for at, k in enumerate(others(step)):
                    here = block_of(vn[k], BACK[k])
                    there = block_of(occ if k == BACK[step] else vn[k], step)
                    pack[axis, at] = jnp.concatenate([here, there], axis=1)

    def along(axis, sign):
        return shifted(0, sign * way, 0) if axis == 0 else shifted(0, 0, sign * way)

    def p_copy(axis):
        gk, ak = along(axis, 1)
        return pltpu.make_async_remote_copy(
            src_ref=pack.at[axis],
            dst_ref=pack.at[2 + axis],
            send_sem=p_send.at[axis],
            recv_sem=p_recv.at[axis],
            device_id={"ao": ak, "grp": gk},
            device_id_type=MESH,
        )

    p_copies = [p_copy(axis) for axis in range(2)]
    for copy in p_copies:
        copy.start()
    lax.fori_loop(first_sends, n_ao - 1, give, 0)

    def mask_lanes(block_step):
        gi, ai = shifted(*block_step)
        on = jnp.zeros((1, width), jnp.int32)
        for j in range(7):
            value = tm_ref[j, gi, ai] * exists(block_step, STEPS[j])
            on = on + jnp.where(lane_block == j, value, 0)
        return on.astype(F32)

    own_lanes = mask_lanes(STEPS[0])
    nothing = jnp.zeros((bs, bs), F32)

    def place(slot, i, k, row_on, lanes_on, block):
        pieces = []
        for j in range(7):
            k2 = second_step(i, j, k)
            pieces.append(nothing if k2 is None else block(k2).astype(F32))
        placed = jnp.concatenate(pieces, axis=1) * lanes_on * row_on
        vs[slot, k * bs : (k + 1) * bs, :] = placed.astype(BF16)

    def place_all(slot_steps):
        lanes = [mask_lanes(STEPS[i]) for _, i in slot_steps]
        for k in range(7):
            row_on = (tm_ref[k, g, a] * exists(STEPS[k])).astype(F32)
            for (slot, i), lanes_on in zip(slot_steps, lanes):
                place(slot, i, k, row_on, lanes_on, lambda k2: block_of(vn[k], k2))

    place_all([(0, 0), (1, 1), (2, 2)])
    for parity in range(2):

        @pl.when(odd == parity)
        def _(parity=parity):
            place_all([(3, BACK[towards(parity, 0)]), (4, BACK[towards(parity, 1)])])

    def source_of(slot, yy, zz):
        turn = slot >> 2
        far = line // 2 - ((turn + 1) >> 1)
        z_from = (zz - far * (2 * (turn & 1) - 1) + line) & (line - 1)
        return ((yy + 1 + (slot & (rows - 1))) & (rows - 1)) * line + z_from

    def spread(yy, zz):
        down = lax.broadcasted_iota(jnp.int32, (tall, bs), 0) // slab
        across = lax.broadcasted_iota(jnp.int32, (bs, tall), 1) // slab
        tall_at = lax.broadcasted_iota(jnp.int32, (tall, bs), 1)
        wide_at = lax.broadcasted_iota(jnp.int32, (bs, tall), 0)
        as_rows = jnp.where(source_of(down, yy, zz) == tall_at, 1.0, 0.0).astype(BF16)
        as_cols = jnp.where(source_of(across, yy, zz) == wide_at, 1.0, 0.0).astype(BF16)
        return as_rows, as_cols

    own_rows, own_cols = spread(y, z)
    y_rows, y_cols = spread((y - way + rows) % rows, z)
    z_rows, z_cols = spread(y, (z - way + line) % line)

    def weigh(slot, as_rows, block, as_cols):
        stretched = jnp.dot(as_rows, block, preferred_element_type=F32).astype(BF16)
        oexp[slot] = jnp.dot(stretched, as_cols, preferred_element_type=F32)

    def by_way(up, down):
        keep = odd.astype(F32)
        both = block_of(occ, up).astype(F32) * (1.0 - keep) + block_of(occ, down).astype(F32) * keep
        return both.astype(BF16)

    weigh(0, own_rows, block_of(occ, 0), own_cols)
    weigh(1, own_rows, block_of(occ, 1), own_cols)
    weigh(2, own_rows, block_of(occ, 2), own_cols)
    weigh(3, own_rows, by_way(3, 4), y_cols)
    weigh(4, own_rows, by_way(5, 6), z_cols)

    for axis in range(2):
        p_copies[axis].wait_recv()
    for parity in range(2):

        @pl.when(odd == parity)
        def _(parity=parity):
            for axis in range(2):
                i = towards(parity, axis)
                ks = others(i)
                source = STEPS[BACK[i]]
                gs, a_s = shifted(*source)
                for k in range(7):
                    row_on = (tm_ref[k, gs, a_s] * exists(source, STEPS[k])).astype(F32)

                    def block(k2, k=k):
                        if k == 0:
                            return block_of(vn[BACK[i]], k2)
                        if k == i:
                            return block_of(vn[0], k2)
                        half = 0 if k2 == BACK[k] else 1
                        return block_of(pack[2 + axis, ks.index(k)], half)

                    place(5 + axis, i, k, row_on, own_lanes, block)
                received = pack[2 + axis, ks.index(BACK[i])]
                as_rows = y_rows if axis == 0 else z_rows
                weigh(5 + axis, as_rows, block_of(received, 1), own_cols)

    chunk = n_ao // PARTS
    high = chunk * slab

    def t_copy(to, p):
        if to < 2:
            gk, ak = shifted(1 - 2 * to, 0, 0)
        else:
            gk, ak = along(to - 2, 1)
        where = pl.ds(p * high, high)
        return pltpu.make_async_remote_copy(
            src_ref=tn.at[0, where],
            dst_ref=tn.at[1 + to, where],
            send_sem=ex_send.at[to, p],
            recv_sem=ex_recv.at[to, p],
            device_id={"ao": ak, "grp": gk},
            device_id_type=MESH,
        )

    t_copies = [[t_copy(to, p) for p in range(PARTS)] for to in range(4)]
    for p in range(PARTS):
        count = chunk if p < PARTS - 1 else chunk - 1
        arrived = arr.at[pl.ds(p * chunk, count)]
        pltpu.make_async_copy(arrived, arrived, a2a_recv.at[p]).wait()
        here = arr[p * chunk : (p + 1) * chunk].astype(F32).reshape(high, width).astype(BF16)
        tn[0, p * high : (p + 1) * high, :] = here
        for to in (3, 2, 1, 0):
            t_copies[to][p].start()
        for s in range(5):
            xs[s, p * high : (p + 1) * high, :] = jnp.dot(
                here, vs[s], preferred_element_type=F32
            ).astype(BF16)

    def pair_sum(slot, left, right, r0, r1_, c0, c1):
        pairs = lax.dot_general(
            left[r0:r1_], right[c0:c1], (((1,), (1,)), ((), ())), preferred_element_type=F32
        )
        weighted = pairs * oexp[slot, r0:r1_, c0:c1]
        summed = jnp.sum(weighted.reshape((r1_ - r0) // slab, slab, c1 - c0), axis=0)
        folded = summed[:, 0:128]
        for at in range(1, (c1 - c0) // 128):
            folded = folded + summed[:, at * 128 : (at + 1) * 128]
        return folded

    part_sum = pair_sum(0, xs.at[0], tn.at[0], 0, tall, 0, tall)
    early = (PARTS - 1) * high
    for lo, hi, parts in ((0, early, range(PARTS - 1)), (early, tall, (PARTS - 1,))):
        for to in (0, 1, 2, 3):
            for p in parts:
                t_copies[to][p].wait_recv()
            part_sum = part_sum + pair_sum(
                1 + to, xs.at[1 + to], tn.at[1 + to], 0, tall, lo, hi
            )
            if to >= 2:
                s = 3 + to
                xs[s, lo:hi, :] = jnp.dot(
                    tn[1 + to, lo:hi, :], vs[s], preferred_element_type=F32
                ).astype(BF16)
                part_sum = part_sum + pair_sum(s, xs.at[s], tn.at[0], lo, hi, 0, tall)

    shift = 64
    while shift >= slab:
        part_sum = part_sum + pltpu.roll(part_sum, shift, 1)
        shift //= 2

    def wait_bytes(buf, count, sem):
        ref = buf.at[pl.ds(0, count - 1)]
        pltpu.make_async_copy(ref, ref, sem).wait()

    def left_all():
        for copy in v_copies + p_copies + [c for per in t_copies for c in per]:
            copy.wait_send()
        wait_bytes(snd, n_ao, a2a_send)

    for p in range(slab):
        psend[p] = part_sum[p : p + 1, :]

    def all_slots(buf, count):
        acc = buf[0]
        for at in range(1, count):
            acc = acc + buf[at]
        return acc

    def to_sheet(d, carry):
        gg = (g + d // rows) % groups
        yy = (y + d % rows) % rows
        pltpu.make_async_remote_copy(
            src_ref=psend.at[gg],
            dst_ref=r1.at[g * rows + y],
            send_sem=r_send.at[0],
            recv_sem=r_recv.at[0],
            device_id={"ao": yy * line + z, "grp": gg},
            device_id_type=MESH,
        ).start()
        return carry

    lax.fori_loop(1, groups * rows, to_sheet, 0)
    r1[g * rows + y] = psend[g]
    wait_bytes(r1, groups * rows, r_recv.at[0])
    r3[z] = all_slots(r1, groups * rows)

    def to_line(d, carry):
        far = line // 2 - d // 2
        zz = (z + far * (2 * (d % 2) - 1) + line) % line
        pltpu.make_async_remote_copy(
            src_ref=r3.at[z],
            dst_ref=r3.at[z],
            send_sem=r_send.at[1],
            recv_sem=r_recv.at[1],
            device_id={"ao": y * line + zz, "grp": g},
            device_id_type=MESH,
        ).start()
        return carry

    lax.fori_loop(1, line, to_line, 0)
    left_all()
    wait_bytes(r1, groups * rows, r_send.at[0])
    wait_bytes(r3, line, r_recv.at[1])
    scale = 1.0 / (bs * math.sqrt(groups * n_ao))
    out_ref[...] = (all_slots(r3, line) * scale)[:, :slab]
    wait_bytes(r3, line, r_send.at[1])


def body(three_center, occ_density, virt_density, tensor_mask, occ_mask, virt_mask, block_sizes):
    groups = lax.axis_size("grp")
    n_ao = lax.axis_size("ao")
    rows = 4
    line = n_ao // rows
    slab = three_center.shape[0]
    bs = occ_density.shape[2]
    width = 7 * bs
    tall = bs * slab
    dims = (groups, rows, line, slab, bs)
    dma = pltpu.SemaphoreType.DMA
    result = pl.pallas_call(
        functools.partial(kernel, dims),
        out_shape=jax.ShapeDtypeStruct((1, slab), F32),
        in_specs=[pl.BlockSpec(memory_space=pltpu.HBM)] * 7,
        out_specs=pl.BlockSpec(memory_space=pltpu.VMEM),
        scratch_shapes=[
            pltpu.VMEM((slab, n_ao, width), BF16),
            pltpu.VMEM((bs, width), BF16),
            pltpu.VMEM((bs, width), BF16),
            pltpu.SMEM((7, groups, n_ao), jnp.int32),
            pltpu.SMEM((7, groups, n_ao), jnp.int32),
            pltpu.SMEM((7, groups, n_ao), jnp.int32),
            pltpu.SMEM((groups, n_ao), jnp.int32),
            dma((7,)),
            pltpu.VMEM((n_ao, slab, width), BF16),
            pltpu.VMEM((n_ao, slab, width), BF16),
            pltpu.VMEM((5, tall, width), BF16),
            pltpu.VMEM((7, bs, width), BF16),
            pltpu.VMEM((4, 5, bs, 2 * bs), BF16),
            pltpu.VMEM((7, width, width), BF16),
            pltpu.VMEM((7, tall, width), BF16),
            pltpu.VMEM((7, tall, tall), F32),
            pltpu.VMEM((slab, 1, 128), F32),
            pltpu.VMEM((groups * rows, 1, 128), F32),
            pltpu.VMEM((line, 1, 128), F32),
            dma,
            dma((PARTS,)),
            dma((4, PARTS)),
            dma((4, PARTS)),
            dma((6,)),
            dma((6,)),
            dma((2,)),
            dma((2,)),
            dma((2,)),
            dma((2,)),
        ],
        compiler_params=pltpu.CompilerParams(
            collective_id=0, has_side_effects=True, vmem_limit_bytes=60 * 1024 * 1024
        ),
    )(
        three_center,
        occ_density.reshape(bs, width),
        virt_density.reshape(bs, width),
        jnp.transpose(tensor_mask, (2, 0, 1)),
        jnp.transpose(occ_mask, (2, 0, 1)),
        jnp.transpose(virt_mask, (2, 0, 1)),
        block_sizes,
    )
    return result


def solution(mesh):
    in_specs = (
        P(None, "grp", "ao"),
        P("grp", "ao", None, None),
        P("grp", "ao", None, None),
        P(),
        P(),
        P(),
        P(),
    )
    return jax.shard_map(
        body, mesh=mesh, in_specs=in_specs, out_specs=P("grp", None), check_vma=False
    )
```

time: 71.5 us -> 68.3 us (0.955)
  Pallas kernels: 70.2 us -> 67 us
    pallas_call x1, Pallas kernels: 70.2 us -> 67 us  [body(): pl.pallas_call(functools.partial(kernel, dims), out_shape=jax.ShapeDtypeS...]
where the time goes in v3:
time: 68.3 us; the launch traced here: 68.2 us
  Pallas kernels  67 us (98%)
  local copies, waits for them, and re-layouts  1.19 us (2%)
    pallas_call x1, Pallas kernels, body(): pl.pallas_call(functools.partial(kernel, dims), out_shape=jax.ShapeDtypeS...  67 us

profile of v3, /device:TPU:1, one launch (start us, length us, event | category | flops | bytes accessed | tf_op | source)
XLA Modules:
  0.0 68.2 jit_solution(14847119802997178402)
XLA Ops:
  0.0 67.0 %shard_map.73 = f32[1,8]{1,0:T(1,128)} custom-call(bf16[8,64,448]{2,1,0:T(8,128)(2,1)} %t_hbm.1, bf16[64,448]{1,0:T(8,128)(2,1)} %bitcast.5, bf16[64,448]{1,0:T(8,128)(2,1)} %bitcast.6, s32[7,8,64]{2,1,0:T(8,128)} %bitcast.7, s32[7,8,64]{2,1,0:T(8,128)} %bitcast.8, s32[7,8,64]{2,1,0:T(8,128)} %bitcast.9, s32[8,64]{1,0:T(8,128)} %sz_hbm.1), custom_call_target="tpu_custom_call" | custom-call | tf_op jit(solution)/shard_map/pallas_call | solution.py:466
  67.0 1.2 %copy.9 = f32[1,8]{1,0:T(1,128)} copy(f32[1,8]{1,0:T(1,128)} %shard_map.73) | data formatting | bytes 64

commit v4 on v3

--- a/solution.py
+++ b/solution.py
@@ -50,8 +50,16 @@
     psend,
     r1,
     r3,
+    y_out,
+    y_in,
+    z_out,
+    tt,
     a2a_send,
     a2a_recv,
+    y_send,
+    y_recv,
+    z_send,
+    z_recv,
     ex_send,
     ex_recv,
     v_send,
@@ -65,6 +73,7 @@
     n_ao = rows * line
     width = 7 * bs
     tall = bs * slab
+    main = width // 128 * 128
     g = lax.axis_index("grp")
     a = lax.axis_index("ao")
     y = a // line
@@ -155,7 +164,13 @@
     for half in range(2):
         rows_in = t_ref[:, half * part : (half + 1) * part, :].reshape(n_rows, width)
         moved_rows = jnp.dot(perm, rows_in, preferred_element_type=F32)
-        snd[half * part : (half + 1) * part] = moved_rows.reshape(part, slab, width).astype(BF16)
+        snd[half * part : (half + 1) * part] = (
+            moved_rows[:, :main].reshape(part, slab, main).astype(BF16)
+        )
+        for at in range(rows // 2):
+            first = moved_rows[at * 2 * bs : at * 2 * bs + bs, main:]
+            second = moved_rows[at * 2 * bs + bs : at * 2 * bs + 2 * bs, main:]
+            y_out[half * (rows // 2) + at] = jnp.concatenate([first, second], axis=1).astype(BF16)
 
     pl.semaphore_wait(barrier, n_ao - 1 + (groups - 1) * rows)
 
@@ -174,11 +189,25 @@
     for copy in v_copies:
         copy.start()
 
+    def give_y(d, carry):
+        y_to = (y + d) % rows
+        pltpu.make_async_remote_copy(
+            src_ref=y_out.at[y_to],
+            dst_ref=y_in.at[y],
+            send_sem=y_send,
+            recv_sem=y_recv,
+            device_id={"ao": y_to * line + z, "grp": g},
+            device_id_type=MESH,
+        ).start()
+        return carry
+
+    lax.fori_loop(1, rows, give_y, 0)
+
     def give(d, carry):
         target = far_first(d)
         pltpu.make_async_remote_copy(
             src_ref=snd.at[target],
-            dst_ref=arr.at[d],
+            dst_ref=arr.at[d // rows * rows + y],
             send_sem=a2a_send,
             recv_sem=a2a_recv.at[d // (n_ao // PARTS)],
             device_id={"ao": target, "grp": g},
@@ -188,11 +217,42 @@
 
     first_sends = n_ao // PARTS
     lax.fori_loop(0, first_sends, give, 0)
-    arr[n_ao - 1] = snd[a]
+    arr[n_ao - rows + y] = snd[a]
+    y_in[y] = y_out[y]
 
     for at in (4, 5, 6):
         loads[at].wait()
     occ = masked(occ_ref[...], om_ref)
+
+    def wait_bytes(buf, count, sem):
+        ref = buf.at[pl.ds(0, count - 1)]
+        pltpu.make_async_copy(ref, ref, sem).wait()
+
+    wait_bytes(y_in, rows, y_recv)
+    for half in range(2):
+        pieces = [y_in[at][:, half * bs : (half + 1) * bs].astype(F32) for at in range(rows)]
+        upper = jnp.concatenate([pieces[0], pieces[2]], axis=1).reshape(line // 2, slab, 2 * bs)
+        lower = jnp.concatenate([pieces[1], pieces[3]], axis=1).reshape(line // 2, slab, 2 * bs)
+        z_out[half * (line // 2) : (half + 1) * (line // 2)] = jnp.concatenate(
+            [upper, lower], axis=1
+        ).astype(BF16)
+    deep = 2 * slab
+
+    def give_z(turn, carry):
+        far = line // 2 - (turn + 1) // 2
+        z_to = (z + far * (2 * (turn % 2) - 1) + line) % line
+        pltpu.make_async_remote_copy(
+            src_ref=z_out.at[z_to],
+            dst_ref=tt.at[0, pl.ds(pl.multiple_of(turn * deep, deep), deep)],
+            send_sem=z_send,
+            recv_sem=z_recv.at[turn // (line // PARTS)],
+            device_id={"ao": y * line + z_to, "grp": g},
+            device_id_type=MESH,
+        ).start()
+        return carry
+
+    lax.fori_loop(0, line - 1, give_z, 0)
+    tt[0, (line - 1) * deep : line * deep] = z_out[z]
 
     for copy in v_copies:
         copy.wait_recv()
@@ -269,24 +329,23 @@
         def _(parity=parity):
             place_all([(3, BACK[towards(parity, 0)]), (4, BACK[towards(parity, 1)])])
 
-    def source_of(slot, yy, zz):
+    def source_of(slot, zz):
         turn = slot >> 2
         far = line // 2 - ((turn + 1) >> 1)
         z_from = (zz - far * (2 * (turn & 1) - 1) + line) & (line - 1)
-        return ((yy + 1 + (slot & (rows - 1))) & (rows - 1)) * line + z_from
-
-    def spread(yy, zz):
+        return (slot & (rows - 1)) * line + z_from
+
+    def spread(zz):
         down = lax.broadcasted_iota(jnp.int32, (tall, bs), 0) // slab
         across = lax.broadcasted_iota(jnp.int32, (bs, tall), 1) // slab
         tall_at = lax.broadcasted_iota(jnp.int32, (tall, bs), 1)
         wide_at = lax.broadcasted_iota(jnp.int32, (bs, tall), 0)
-        as_rows = jnp.where(source_of(down, yy, zz) == tall_at, 1.0, 0.0).astype(BF16)
-        as_cols = jnp.where(source_of(across, yy, zz) == wide_at, 1.0, 0.0).astype(BF16)
+        as_rows = jnp.where(source_of(down, zz) == tall_at, 1.0, 0.0).astype(BF16)
+        as_cols = jnp.where(source_of(across, zz) == wide_at, 1.0, 0.0).astype(BF16)
         return as_rows, as_cols
 
-    own_rows, own_cols = spread(y, z)
-    y_rows, y_cols = spread((y - way + rows) % rows, z)
-    z_rows, z_cols = spread(y, (z - way + line) % line)
+    own_rows, own_cols = spread(z)
+    z_rows, z_cols = spread((z - way + line) % line)
 
     def weigh(slot, as_rows, block, as_cols):
         stretched = jnp.dot(as_rows, block, preferred_element_type=F32).astype(BF16)
@@ -300,7 +359,7 @@
     weigh(0, own_rows, block_of(occ, 0), own_cols)
     weigh(1, own_rows, block_of(occ, 1), own_cols)
     weigh(2, own_rows, block_of(occ, 2), own_cols)
-    weigh(3, own_rows, by_way(3, 4), y_cols)
+    weigh(3, own_rows, by_way(3, 4), own_cols)
     weigh(4, own_rows, by_way(5, 6), z_cols)
 
     for axis in range(2):
@@ -327,36 +386,56 @@
 
                     place(5 + axis, i, k, row_on, own_lanes, block)
                 received = pack[2 + axis, ks.index(BACK[i])]
-                as_rows = y_rows if axis == 0 else z_rows
+                as_rows = own_rows if axis == 0 else z_rows
                 weigh(5 + axis, as_rows, block_of(received, 1), own_cols)
 
     chunk = n_ao // PARTS
     high = chunk * slab
 
-    def t_copy(to, p):
+    def t_copy(to, p, lanes):
         if to < 2:
             gk, ak = shifted(1 - 2 * to, 0, 0)
         else:
             gk, ak = along(to - 2, 1)
-        where = pl.ds(p * high, high)
+        if lanes:
+            here = tn.at[0, pl.ds(p * high, high), pl.ds(0, main)]
+            there = tn.at[1 + to, pl.ds(p * high, high), pl.ds(0, main)]
+        else:
+            here = tt.at[0, pl.ds(p * high // 2, high // 2)]
+            there = tt.at[1 + to, pl.ds(p * high // 2, high // 2)]
         return pltpu.make_async_remote_copy(
-            src_ref=tn.at[0, where],
-            dst_ref=tn.at[1 + to, where],
-            send_sem=ex_send.at[to, p],
-            recv_sem=ex_recv.at[to, p],
+            src_ref=here,
+            dst_ref=there,
+            send_sem=ex_send.at[to, p, lanes],
+            recv_sem=ex_recv.at[to, p, lanes],
             device_id={"ao": ak, "grp": gk},
             device_id_type=MESH,
         )
 
-    t_copies = [[t_copy(to, p) for p in range(PARTS)] for to in range(4)]
+    t_copies = [[[t_copy(to, p, lanes) for lanes in range(2)] for p in range(PARTS)] for to in range(4)]
+
+    def unpack_tail(at, p):
+        last = tt[at, p * high // 2 : (p + 1) * high // 2, :].astype(F32)
+        last = last.reshape(line // PARTS, deep, 2 * bs)
+        both = jnp.concatenate([last[:, :, :bs], last[:, :, bs:]], axis=1)
+        tn[at, p * high : (p + 1) * high, main:] = both.reshape(high, bs).astype(BF16)
+
     for p in range(PARTS):
         count = chunk if p < PARTS - 1 else chunk - 1
         arrived = arr.at[pl.ds(p * chunk, count)]
         pltpu.make_async_copy(arrived, arrived, a2a_recv.at[p]).wait()
-        here = arr[p * chunk : (p + 1) * chunk].astype(F32).reshape(high, width).astype(BF16)
-        tn[0, p * high : (p + 1) * high, :] = here
+        tn[0, p * high : (p + 1) * high, :main] = (
+            arr[p * chunk : (p + 1) * chunk].astype(F32).reshape(high, main).astype(BF16)
+        )
         for to in (3, 2, 1, 0):
-            t_copies[to][p].start()
+            t_copies[to][p][1].start()
+        turns = line // PARTS if p < PARTS - 1 else line // PARTS - 1
+        arrived = tt.at[0, pl.ds(p * high // 2, turns * deep)]
+        pltpu.make_async_copy(arrived, arrived, z_recv.at[p]).wait()
+        for to in (3, 2, 1, 0):
+            t_copies[to][p][0].start()
+        unpack_tail(0, p)
+        here = tn[0, p * high : (p + 1) * high, :]
         for s in range(5):
             xs[s, p * high : (p + 1) * high, :] = jnp.dot(
                 here, vs[s], preferred_element_type=F32
@@ -378,7 +457,9 @@
     for lo, hi, parts in ((0, early, range(PARTS - 1)), (early, tall, (PARTS - 1,))):
         for to in (0, 1, 2, 3):
             for p in parts:
-                t_copies[to][p].wait_recv()
+                for copy in t_copies[to][p]:
+                    copy.wait_recv()
+                unpack_tail(1 + to, p)
             part_sum = part_sum + pair_sum(
                 1 + to, xs.at[1 + to], tn.at[1 + to], 0, tall, lo, hi
             )
@@ -394,14 +475,12 @@
         part_sum = part_sum + pltpu.roll(part_sum, shift, 1)
         shift //= 2
 
-    def wait_bytes(buf, count, sem):
-        ref = buf.at[pl.ds(0, count - 1)]
-        pltpu.make_async_copy(ref, ref, sem).wait()
-
     def left_all():
-        for copy in v_copies + p_copies + [c for per in t_copies for c in per]:
+        for copy in v_copies + p_copies + [c for per in t_copies for two in per for c in two]:
             copy.wait_send()
         wait_bytes(snd, n_ao, a2a_send)
+        wait_bytes(y_out, rows, y_send)
+        wait_bytes(z_out, line, z_send)
 
     for p in range(slab):
         psend[p] = part_sum[p : p + 1, :]
@@ -477,8 +556,8 @@
             pltpu.SMEM((7, groups, n_ao), jnp.int32),
             pltpu.SMEM((groups, n_ao), jnp.int32),
             dma((7,)),
-            pltpu.VMEM((n_ao, slab, width), BF16),
-            pltpu.VMEM((n_ao, slab, width), BF16),
+            pltpu.VMEM((n_ao, slab, width // 128 * 128), BF16),
+            pltpu.VMEM((n_ao, slab, width // 128 * 128), BF16),
             pltpu.VMEM((5, tall, width), BF16),
             pltpu.VMEM((7, bs, width), BF16),
             pltpu.VMEM((4, 5, bs, 2 * bs), BF16),
@@ -488,10 +567,18 @@
             pltpu.VMEM((slab, 1, 128), F32),
             pltpu.VMEM((groups * rows, 1, 128), F32),
             pltpu.VMEM((line, 1, 128), F32),
+            pltpu.VMEM((rows, bs, 2 * bs), BF16),
+            pltpu.VMEM((rows, bs, 2 * bs), BF16),
+            pltpu.VMEM((line, 2 * slab, 2 * bs), BF16),
+            pltpu.VMEM((5, line * 2 * slab, 2 * bs), BF16),
             dma,
             dma((PARTS,)),
-            dma((4, PARTS)),
-            dma((4, PARTS)),
+            dma,
+            dma,
+            dma,
+            dma((PARTS,)),
+            dma((4, PARTS, 2)),
+            dma((4, PARTS, 2)),
             dma((6,)),
             dma((6,)),
             dma((2,)),

time: 68.3 us -> 66.2 us (0.969)
  Pallas kernels: 67 us -> 64.8 us
    pallas_call x1, Pallas kernels: 67 us -> 64.8 us  [body(): pl.pallas_call(functools.partial(kernel, dims), out_shape=jax.ShapeDtypeS...]
where the time goes in v4:
time: 66.2 us; the launch traced here: 66 us
  Pallas kernels  64.8 us (98%)
  local copies, waits for them, and re-layouts  1.19 us (2%)
    pallas_call x1, Pallas kernels, body(): pl.pallas_call(functools.partial(kernel, dims), out_shape=jax.ShapeDtypeS...  64.8 us

profile of v4, /device:TPU:1, one launch (start us, length us, event | category | flops | bytes accessed | tf_op | source)
XLA Modules:
  0.0 66.0 jit_solution(12482383931173686246)
XLA Ops:
  0.0 64.8 %shard_map.73 = f32[1,8]{1,0:T(1,128)} custom-call(bf16[8,64,448]{2,1,0:T(8,128)(2,1)} %t_hbm.1, bf16[64,448]{1,0:T(8,128)(2,1)} %bitcast.5, bf16[64,448]{1,0:T(8,128)(2,1)} %bitcast.6, s32[7,8,64]{2,1,0:T(8,128)} %bitcast.7, s32[7,8,64]{2,1,0:T(8,128)} %bitcast.8, s32[7,8,64]{2,1,0:T(8,128)} %bitcast.9, s32[8,64]{1,0:T(8,128)} %sz_hbm.1), custom_call_target="tpu_custom_call" | custom-call | tf_op jit(solution)/shard_map/pallas_call | solution.py:545
  64.8 1.2 %copy.9 = f32[1,8]{1,0:T(1,128)} copy(f32[1,8]{1,0:T(1,128)} %shard_map.73) | data formatting | bytes 64

commit v5 on v4

--- a/solution.py
+++ b/solution.py
@@ -94,33 +94,6 @@
         inside = (gg >= 0) & (gg < groups) & (yy >= 0) & (yy < rows) & (zz >= 0) & (zz < line)
         return inside.astype(jnp.int32)
 
-    barrier = pltpu.get_barrier_semaphore()
-
-    def far_first(d):
-        turn = d // rows
-        far = line // 2 - (turn + 1) // 2
-        z_to = (z + far * (2 * (turn % 2) - 1) + line) % line
-        y_to = (y + rows - 1 - d % rows) % rows
-        return y_to * line + z_to
-
-    def greet_ao(d, carry):
-        pl.semaphore_signal(
-            barrier, inc=1, device_id={"ao": far_first(d), "grp": g}, device_id_type=MESH
-        )
-        return carry
-
-    lax.fori_loop(0, n_ao - 1, greet_ao, 0)
-
-    def greet_sheet(d, carry):
-        gg = (g + 1 + d // rows) % groups
-        yy = (y + d) % rows
-        pl.semaphore_signal(
-            barrier, inc=1, device_id={"ao": yy * line + z, "grp": gg}, device_id_type=MESH
-        )
-        return carry
-
-    lax.fori_loop(0, (groups - 1) * rows, greet_sheet, 0)
-
     loads = []
     for at, (source, target) in enumerate(
         (
@@ -135,6 +108,42 @@
     ):
         loads.append(pltpu.make_async_copy(source, target, load_sem.at[at]))
         loads[-1].start()
+
+    barrier = pltpu.get_barrier_semaphore()
+    half_line = line // 2
+    y_at = [lax.rem(y + rows - 1 - q, rows) for q in range(rows)]
+    across_line = lax.rem(z + half_line, line)
+
+    def both_ways(i):
+        far = half_line - i
+        return (
+            (lax.rem(z + far, line), 2 * i - 1),
+            (lax.rem(z - far + line, line), 2 * i),
+        )
+
+    def greet(aa, gg):
+        pl.semaphore_signal(barrier, inc=1, device_id={"ao": aa, "grp": gg}, device_id_type=MESH)
+
+    for q in range(rows):
+        greet(y_at[q] * line + across_line, g)
+
+    def greet_ao(i, carry):
+        for z_to, _ in both_ways(i):
+            for q in range(rows):
+                greet(y_at[q] * line + z_to, g)
+        return carry
+
+    lax.fori_loop(1, half_line, greet_ao, 0)
+    for q in range(rows - 1):
+        greet(y_at[q] * line + z, g)
+
+    def greet_sheet(d, carry):
+        gg = lax.rem(g + d, groups)
+        for q in range(rows):
+            greet(y_at[q] * line + z, gg)
+        return carry
+
+    lax.fori_loop(1, groups, greet_sheet, 0)
 
     lane = lax.broadcasted_iota(jnp.int32, (1, width), 1)
     lane_block = lane // bs
@@ -185,38 +194,49 @@
             device_id_type=MESH,
         )
 
+    def give_y(q):
+        return pltpu.make_async_remote_copy(
+            src_ref=y_out.at[y_at[q]],
+            dst_ref=y_in.at[y],
+            send_sem=y_send,
+            recv_sem=y_recv,
+            device_id={"ao": y_at[q] * line + z, "grp": g},
+            device_id_type=MESH,
+        )
+
+    for q in range(rows - 1):
+        give_y(q).start()
+
+    def place_at(steps):
+        return lax.rem(z + way * steps + line, line)
+
+    def give(turn, z_to, z_block, count=rows):
+        for q in range(count):
+            pltpu.make_async_remote_copy(
+                src_ref=snd.at[y_at[q] * line + z_block],
+                dst_ref=arr.at[turn * rows + y],
+                send_sem=a2a_send,
+                recv_sem=a2a_recv.at[turn // (line // PARTS)],
+                device_id={"ao": y_at[q] * line + z_to, "grp": g},
+                device_id_type=MESH,
+            ).start()
+
+    def give_ahead(turn, carry):
+        far = half_line - 1 - turn
+        give(turn, place_at(-far), place_at(-far - 1))
+        return carry
+
+    def give_own(turn, carry):
+        z_to = place_at(line - 1 - turn)
+        give(turn, z_to, z_to)
+        return carry
+
+    give_ahead(0, 0)
+    give_ahead(1, 0)
     v_copies = [v_copy(k) for k in range(1, 7)]
     for copy in v_copies:
         copy.start()
-
-    def give_y(d, carry):
-        y_to = (y + d) % rows
-        pltpu.make_async_remote_copy(
-            src_ref=y_out.at[y_to],
-            dst_ref=y_in.at[y],
-            send_sem=y_send,
-            recv_sem=y_recv,
-            device_id={"ao": y_to * line + z, "grp": g},
-            device_id_type=MESH,
-        ).start()
-        return carry
-
-    lax.fori_loop(1, rows, give_y, 0)
-
-    def give(d, carry):
-        target = far_first(d)
-        pltpu.make_async_remote_copy(
-            src_ref=snd.at[target],
-            dst_ref=arr.at[d // rows * rows + y],
-            send_sem=a2a_send,
-            recv_sem=a2a_recv.at[d // (n_ao // PARTS)],
-            device_id={"ao": target, "grp": g},
-            device_id_type=MESH,
-        ).start()
-        return carry
-
-    first_sends = n_ao // PARTS
-    lax.fori_loop(0, first_sends, give, 0)
+    arr[(half_line - 1) * rows + y] = snd[y * line + place_at(-1)]
     arr[n_ao - rows + y] = snd[a]
     y_in[y] = y_out[y]
 
@@ -238,20 +258,29 @@
         ).astype(BF16)
     deep = 2 * slab
 
-    def give_z(turn, carry):
-        far = line // 2 - (turn + 1) // 2
-        z_to = (z + far * (2 * (turn % 2) - 1) + line) % line
+    def give_z(slot, turn, z_to, z_block):
         pltpu.make_async_remote_copy(
-            src_ref=z_out.at[z_to],
-            dst_ref=tt.at[0, pl.ds(pl.multiple_of(turn * deep, deep), deep)],
+            src_ref=z_out.at[z_block],
+            dst_ref=tt.at[slot, pl.ds(pl.multiple_of(turn * deep, deep), deep)],
             send_sem=z_send,
             recv_sem=z_recv.at[turn // (line // PARTS)],
             device_id={"ao": y * line + z_to, "grp": g},
             device_id_type=MESH,
         ).start()
+
+    def give_z_ahead(turn, carry):
+        far = half_line - 1 - turn
+        give_z(4, turn, place_at(-far), place_at(-far - 1))
         return carry
 
-    lax.fori_loop(0, line - 1, give_z, 0)
+    def give_z_own(turn, carry):
+        z_to = place_at(line - 1 - turn)
+        give_z(0, turn, z_to, z_to)
+        return carry
+
+    lax.fori_loop(0, half_line - 1, give_z_ahead, 0)
+    lax.fori_loop(half_line, line - 1, give_z_own, 0)
+    tt[4, (half_line - 1) * deep : half_line * deep] = z_out[place_at(-1)]
     tt[0, (line - 1) * deep : line * deep] = z_out[z]
 
     for copy in v_copies:
@@ -294,7 +323,10 @@
     p_copies = [p_copy(axis) for axis in range(2)]
     for copy in p_copies:
         copy.start()
-    lax.fori_loop(first_sends, n_ao - 1, give, 0)
+    lax.fori_loop(2, half_line - 1, give_ahead, 0)
+    give(half_line - 1, z, place_at(-1), rows - 1)
+    lax.fori_loop(half_line, line - 1, give_own, 0)
+    give(line - 1, z, z, rows - 1)
 
     def mask_lanes(block_step):
         gi, ai = shifted(*block_step)
@@ -329,23 +361,23 @@
         def _(parity=parity):
             place_all([(3, BACK[towards(parity, 0)]), (4, BACK[towards(parity, 1)])])
 
-    def source_of(slot, zz):
+    def source_of(slot, zz, ww):
         turn = slot >> 2
-        far = line // 2 - ((turn + 1) >> 1)
-        z_from = (zz - far * (2 * (turn & 1) - 1) + line) & (line - 1)
-        return (slot & (rows - 1)) * line + z_from
-
-    def spread(zz):
+        ahead = jnp.where(turn < half_line, half_line - turn, turn - (line - 1))
+        return (slot & (rows - 1)) * line + ((zz + ww * ahead + line) & (line - 1))
+
+    def spread(zz, ww):
         down = lax.broadcasted_iota(jnp.int32, (tall, bs), 0) // slab
         across = lax.broadcasted_iota(jnp.int32, (bs, tall), 1) // slab
         tall_at = lax.broadcasted_iota(jnp.int32, (tall, bs), 1)
         wide_at = lax.broadcasted_iota(jnp.int32, (bs, tall), 0)
-        as_rows = jnp.where(source_of(down, zz) == tall_at, 1.0, 0.0).astype(BF16)
-        as_cols = jnp.where(source_of(across, zz) == wide_at, 1.0, 0.0).astype(BF16)
+        as_rows = jnp.where(source_of(down, zz, ww) == tall_at, 1.0, 0.0).astype(BF16)
+        as_cols = jnp.where(source_of(across, zz, ww) == wide_at, 1.0, 0.0).astype(BF16)
         return as_rows, as_cols
 
-    own_rows, own_cols = spread(z)
-    z_rows, z_cols = spread((z - way + line) % line)
+    own_rows, own_cols = spread(z, way)
+    x_cols = spread(z, -way)[1]
+    z_rows, z_cols = spread(place_at(-1), way)
 
     def weigh(slot, as_rows, block, as_cols):
         stretched = jnp.dot(as_rows, block, preferred_element_type=F32).astype(BF16)
@@ -357,8 +389,8 @@
         return both.astype(BF16)
 
     weigh(0, own_rows, block_of(occ, 0), own_cols)
-    weigh(1, own_rows, block_of(occ, 1), own_cols)
-    weigh(2, own_rows, block_of(occ, 2), own_cols)
+    weigh(1, own_rows, block_of(occ, 1), x_cols)
+    weigh(2, own_rows, block_of(occ, 2), x_cols)
     weigh(3, own_rows, by_way(3, 4), own_cols)
     weigh(4, own_rows, by_way(5, 6), z_cols)
 
@@ -393,16 +425,20 @@
     high = chunk * slab
 
     def t_copy(to, p, lanes):
+        source, target = 0, 1 + to
         if to < 2:
             gk, ak = shifted(1 - 2 * to, 0, 0)
+        elif to == 3 and p < PARTS // 2:
+            gk, ak = along(1, -1)
+            source, target = target, source
         else:
             gk, ak = along(to - 2, 1)
         if lanes:
-            here = tn.at[0, pl.ds(p * high, high), pl.ds(0, main)]
-            there = tn.at[1 + to, pl.ds(p * high, high), pl.ds(0, main)]
+            here = tn.at[source, pl.ds(p * high, high), pl.ds(0, main)]
+            there = tn.at[target, pl.ds(p * high, high), pl.ds(0, main)]
         else:
-            here = tt.at[0, pl.ds(p * high // 2, high // 2)]
-            there = tt.at[1 + to, pl.ds(p * high // 2, high // 2)]
+            here = tt.at[source, pl.ds(p * high // 2, high // 2)]
+            there = tt.at[target, pl.ds(p * high // 2, high // 2)]
         return pltpu.make_async_remote_copy(
             src_ref=here,
             dst_ref=there,
@@ -420,31 +456,37 @@
         both = jnp.concatenate([last[:, :, :bs], last[:, :, bs:]], axis=1)
         tn[at, p * high : (p + 1) * high, main:] = both.reshape(high, bs).astype(BF16)
 
-    for p in range(PARTS):
-        count = chunk if p < PARTS - 1 else chunk - 1
-        arrived = arr.at[pl.ds(p * chunk, count)]
+    def take_part(p, slot, on_to):
+        lacks = p % 2
+        arrived = arr.at[pl.ds(p * chunk, chunk - lacks)]
         pltpu.make_async_copy(arrived, arrived, a2a_recv.at[p]).wait()
-        tn[0, p * high : (p + 1) * high, :main] = (
+        tn[slot, p * high : (p + 1) * high, :main] = (
             arr[p * chunk : (p + 1) * chunk].astype(F32).reshape(high, main).astype(BF16)
         )
-        for to in (3, 2, 1, 0):
+        for to in on_to:
             t_copies[to][p][1].start()
-        turns = line // PARTS if p < PARTS - 1 else line // PARTS - 1
-        arrived = tt.at[0, pl.ds(p * high // 2, turns * deep)]
+        arrived = tt.at[slot, pl.ds(p * high // 2, (line // PARTS - lacks) * deep)]
         pltpu.make_async_copy(arrived, arrived, z_recv.at[p]).wait()
-        for to in (3, 2, 1, 0):
+        for to in on_to:
             t_copies[to][p][0].start()
+        unpack_tail(slot, p)
+
+    for p in range(PARTS // 2):
+        take_part(p, 4, (3,))
+    for p in range(PARTS // 2):
+        for lanes in (1, 0):
+            t_copies[3][p][lanes].wait_recv()
+            for to in (2, 1, 0):
+                t_copies[to][p][lanes].start()
         unpack_tail(0, p)
-        here = tn[0, p * high : (p + 1) * high, :]
-        for s in range(5):
-            xs[s, p * high : (p + 1) * high, :] = jnp.dot(
-                here, vs[s], preferred_element_type=F32
-            ).astype(BF16)
+    for p in range(PARTS // 2, PARTS):
+        take_part(p, 0, (3, 2, 1, 0))
+
+    for s in range(5):
+        xs[s] = jnp.dot(tn[0], vs[s], preferred_element_type=F32).astype(BF16)
 
     def pair_sum(slot, left, right, r0, r1_, c0, c1):
-        pairs = lax.dot_general(
-            left[r0:r1_], right[c0:c1], (((1,), (1,)), ((), ())), preferred_element_type=F32
-        )
+        pairs = lax.dot_general(left, right, (((1,), (1,)), ((), ())), preferred_element_type=F32)
         weighted = pairs * oexp[slot, r0:r1_, c0:c1]
         summed = jnp.sum(weighted.reshape((r1_ - r0) // slab, slab, c1 - c0), axis=0)
         folded = summed[:, 0:128]
@@ -452,23 +494,29 @@
             folded = folded + summed[:, at * 128 : (at + 1) * 128]
         return folded
 
-    part_sum = pair_sum(0, xs.at[0], tn.at[0], 0, tall, 0, tall)
+    part_sum = pair_sum(0, xs[0], tn[0], 0, tall, 0, tall)
     early = (PARTS - 1) * high
     for lo, hi, parts in ((0, early, range(PARTS - 1)), (early, tall, (PARTS - 1,))):
         for to in (0, 1, 2, 3):
             for p in parts:
-                for copy in t_copies[to][p]:
-                    copy.wait_recv()
-                unpack_tail(1 + to, p)
+                if to < 3 or p >= PARTS // 2:
+                    for copy in t_copies[to][p]:
+                        copy.wait_recv()
+        for to in (0, 1, 2, 3):
+            for p in parts:
+                if to < 3 or p >= PARTS // 2:
+                    unpack_tail(1 + to, p)
+        both = {}
+        for to in (2, 3):
+            both[to] = jnp.dot(
+                tn[1 + to, lo:hi, :], vs[3 + to], preferred_element_type=F32
+            ).astype(BF16)
+        for to in (0, 1, 2, 3):
             part_sum = part_sum + pair_sum(
-                1 + to, xs.at[1 + to], tn.at[1 + to], 0, tall, lo, hi
+                1 + to, xs[1 + to], tn[1 + to, lo:hi, :], 0, tall, lo, hi
             )
-            if to >= 2:
-                s = 3 + to
-                xs[s, lo:hi, :] = jnp.dot(
-                    tn[1 + to, lo:hi, :], vs[s], preferred_element_type=F32
-                ).astype(BF16)
-                part_sum = part_sum + pair_sum(s, xs.at[s], tn.at[0], lo, hi, 0, tall)
+        for to in (2, 3):
+            part_sum = part_sum + pair_sum(3 + to, both[to], tn[0], lo, hi, 0, tall)
 
     shift = 64
     while shift >= slab:
@@ -478,9 +526,9 @@
     def left_all():
         for copy in v_copies + p_copies + [c for per in t_copies for two in per for c in two]:
             copy.wait_send()
-        wait_bytes(snd, n_ao, a2a_send)
+        wait_bytes(snd, n_ao - 1, a2a_send)
         wait_bytes(y_out, rows, y_send)
-        wait_bytes(z_out, line, z_send)
+        wait_bytes(z_out, line - 1, z_send)
 
     for p in range(slab):
         psend[p] = part_sum[p : p + 1, :]
@@ -491,38 +539,39 @@
             acc = acc + buf[at]
         return acc
 
-    def to_sheet(d, carry):
-        gg = (g + d // rows) % groups
-        yy = (y + d % rows) % rows
-        pltpu.make_async_remote_copy(
-            src_ref=psend.at[gg],
-            dst_ref=r1.at[g * rows + y],
-            send_sem=r_send.at[0],
-            recv_sem=r_recv.at[0],
-            device_id={"ao": yy * line + z, "grp": gg},
-            device_id_type=MESH,
-        ).start()
-        return carry
-
-    lax.fori_loop(1, groups * rows, to_sheet, 0)
+    for dg in (4, 3, 5, 2, 6, 1, 7, 0):
+        gg = lax.rem(g + dg, groups)
+        for q in (1, 0, 2, 3):
+            if dg or q < rows - 1:
+                pltpu.make_async_remote_copy(
+                    src_ref=psend.at[gg],
+                    dst_ref=r1.at[g * rows + y],
+                    send_sem=r_send.at[0],
+                    recv_sem=r_recv.at[0],
+                    device_id={"ao": y_at[q] * line + z, "grp": gg},
+                    device_id_type=MESH,
+                ).start()
     r1[g * rows + y] = psend[g]
     wait_bytes(r1, groups * rows, r_recv.at[0])
     r3[z] = all_slots(r1, groups * rows)
 
-    def to_line(d, carry):
-        far = line // 2 - d // 2
-        zz = (z + far * (2 * (d % 2) - 1) + line) % line
+    def to_line(z_to):
         pltpu.make_async_remote_copy(
             src_ref=r3.at[z],
             dst_ref=r3.at[z],
             send_sem=r_send.at[1],
             recv_sem=r_recv.at[1],
-            device_id={"ao": y * line + zz, "grp": g},
+            device_id={"ao": y * line + z_to, "grp": g},
             device_id_type=MESH,
         ).start()
+
+    def to_both_ways(i, carry):
+        for z_to, _ in both_ways(i):
+            to_line(z_to)
         return carry
 
-    lax.fori_loop(1, line, to_line, 0)
+    to_line(across_line)
+    lax.fori_loop(1, half_line, to_both_ways, 0)
     left_all()
     wait_bytes(r1, groups * rows, r_send.at[0])
     wait_bytes(r3, line, r_recv.at[1])
@@ -562,7 +611,7 @@
             pltpu.VMEM((7, bs, width), BF16),
             pltpu.VMEM((4, 5, bs, 2 * bs), BF16),
             pltpu.VMEM((7, width, width), BF16),
-            pltpu.VMEM((7, tall, width), BF16),
+            pltpu.VMEM((5, tall, width), BF16),
             pltpu.VMEM((7, tall, tall), F32),
             pltpu.VMEM((slab, 1, 128), F32),
             pltpu.VMEM((groups * rows, 1, 128), F32),

time: 66.2 us -> 64.6 us (0.976)
  Pallas kernels: 64.8 us -> 63.2 us
    pallas_call x1, Pallas kernels: 64.8 us -> 63.2 us  [body(): pl.pallas_call(functools.partial(kernel, dims), out_shape=jax.ShapeDtypeS...]
where the time goes in v5:
time: 64.6 us; the launch traced here: 64.4 us
  Pallas kernels  63.2 us (98%)
  local copies, waits for them, and re-layouts  1.19 us (2%)
    pallas_call x1, Pallas kernels, body(): pl.pallas_call(functools.partial(kernel, dims), out_shape=jax.ShapeDtypeS...  63.2 us

profile of v5, /device:TPU:1, one launch (start us, length us, event | category | flops | bytes accessed | tf_op | source)
XLA Modules:
  0.0 64.4 jit_solution(9434223840180665967)
XLA Ops:
  0.0 63.2 %shard_map.73 = f32[1,8]{1,0:T(1,128)} custom-call(bf16[8,64,448]{2,1,0:T(8,128)(2,1)} %t_hbm.1, bf16[64,448]{1,0:T(8,128)(2,1)} %bitcast.5, bf16[64,448]{1,0:T(8,128)(2,1)} %bitcast.6, s32[7,8,64]{2,1,0:T(8,128)} %bitcast.7, s32[7,8,64]{2,1,0:T(8,128)} %bitcast.8, s32[7,8,64]{2,1,0:T(8,128)} %bitcast.9, s32[8,64]{1,0:T(8,128)} %sz_hbm.1), custom_call_target="tpu_custom_call" | custom-call | tf_op jit(solution)/shard_map/pallas_call | solution.py:594
  63.3 1.2 %copy.9 = f32[1,8]{1,0:T(1,128)} copy(f32[1,8]{1,0:T(1,128)} %shard_map.73) | data formatting | bytes 64

commit v6 on v5

--- a/solution.py
+++ b/solution.py
@@ -231,11 +231,10 @@
         give(turn, z_to, z_to)
         return carry
 
-    give_ahead(0, 0)
-    give_ahead(1, 0)
     v_copies = [v_copy(k) for k in range(1, 7)]
     for copy in v_copies:
         copy.start()
+    lax.fori_loop(0, 4, give_ahead, 0)
     arr[(half_line - 1) * rows + y] = snd[y * line + place_at(-1)]
     arr[n_ao - rows + y] = snd[a]
     y_in[y] = y_out[y]
@@ -323,103 +322,8 @@
     p_copies = [p_copy(axis) for axis in range(2)]
     for copy in p_copies:
         copy.start()
-    lax.fori_loop(2, half_line - 1, give_ahead, 0)
+    lax.fori_loop(4, half_line - 1, give_ahead, 0)
     give(half_line - 1, z, place_at(-1), rows - 1)
-    lax.fori_loop(half_line, line - 1, give_own, 0)
-    give(line - 1, z, z, rows - 1)
-
-    def mask_lanes(block_step):
-        gi, ai = shifted(*block_step)
-        on = jnp.zeros((1, width), jnp.int32)
-        for j in range(7):
-            value = tm_ref[j, gi, ai] * exists(block_step, STEPS[j])
-            on = on + jnp.where(lane_block == j, value, 0)
-        return on.astype(F32)
-
-    own_lanes = mask_lanes(STEPS[0])
-    nothing = jnp.zeros((bs, bs), F32)
-
-    def place(slot, i, k, row_on, lanes_on, block):
-        pieces = []
-        for j in range(7):
-            k2 = second_step(i, j, k)
-            pieces.append(nothing if k2 is None else block(k2).astype(F32))
-        placed = jnp.concatenate(pieces, axis=1) * lanes_on * row_on
-        vs[slot, k * bs : (k + 1) * bs, :] = placed.astype(BF16)
-
-    def place_all(slot_steps):
-        lanes = [mask_lanes(STEPS[i]) for _, i in slot_steps]
-        for k in range(7):
-            row_on = (tm_ref[k, g, a] * exists(STEPS[k])).astype(F32)
-            for (slot, i), lanes_on in zip(slot_steps, lanes):
-                place(slot, i, k, row_on, lanes_on, lambda k2: block_of(vn[k], k2))
-
-    place_all([(0, 0), (1, 1), (2, 2)])
-    for parity in range(2):
-
-        @pl.when(odd == parity)
-        def _(parity=parity):
-            place_all([(3, BACK[towards(parity, 0)]), (4, BACK[towards(parity, 1)])])
-
-    def source_of(slot, zz, ww):
-        turn = slot >> 2
-        ahead = jnp.where(turn < half_line, half_line - turn, turn - (line - 1))
-        return (slot & (rows - 1)) * line + ((zz + ww * ahead + line) & (line - 1))
-
-    def spread(zz, ww):
-        down = lax.broadcasted_iota(jnp.int32, (tall, bs), 0) // slab
-        across = lax.broadcasted_iota(jnp.int32, (bs, tall), 1) // slab
-        tall_at = lax.broadcasted_iota(jnp.int32, (tall, bs), 1)
-        wide_at = lax.broadcasted_iota(jnp.int32, (bs, tall), 0)
-        as_rows = jnp.where(source_of(down, zz, ww) == tall_at, 1.0, 0.0).astype(BF16)
-        as_cols = jnp.where(source_of(across, zz, ww) == wide_at, 1.0, 0.0).astype(BF16)
-        return as_rows, as_cols
-
-    own_rows, own_cols = spread(z, way)
-    x_cols = spread(z, -way)[1]
-    z_rows, z_cols = spread(place_at(-1), way)
-
-    def weigh(slot, as_rows, block, as_cols):
-        stretched = jnp.dot(as_rows, block, preferred_element_type=F32).astype(BF16)
-        oexp[slot] = jnp.dot(stretched, as_cols, preferred_element_type=F32)
-
-    def by_way(up, down):
-        keep = odd.astype(F32)
-        both = block_of(occ, up).astype(F32) * (1.0 - keep) + block_of(occ, down).astype(F32) * keep
-        return both.astype(BF16)
-
-    weigh(0, own_rows, block_of(occ, 0), own_cols)
-    weigh(1, own_rows, block_of(occ, 1), x_cols)
-    weigh(2, own_rows, block_of(occ, 2), x_cols)
-    weigh(3, own_rows, by_way(3, 4), own_cols)
-    weigh(4, own_rows, by_way(5, 6), z_cols)
-
-    for axis in range(2):
-        p_copies[axis].wait_recv()
-    for parity in range(2):
-
-        @pl.when(odd == parity)
-        def _(parity=parity):
-            for axis in range(2):
-                i = towards(parity, axis)
-                ks = others(i)
-                source = STEPS[BACK[i]]
-                gs, a_s = shifted(*source)
-                for k in range(7):
-                    row_on = (tm_ref[k, gs, a_s] * exists(source, STEPS[k])).astype(F32)
-
-                    def block(k2, k=k):
-                        if k == 0:
-                            return block_of(vn[BACK[i]], k2)
-                        if k == i:
-                            return block_of(vn[0], k2)
-                        half = 0 if k2 == BACK[k] else 1
-                        return block_of(pack[2 + axis, ks.index(k)], half)
-
-                    place(5 + axis, i, k, row_on, own_lanes, block)
-                received = pack[2 + axis, ks.index(BACK[i])]
-                as_rows = own_rows if axis == 0 else z_rows
-                weigh(5 + axis, as_rows, block_of(received, 1), own_cols)
 
     chunk = n_ao // PARTS
     high = chunk * slab
@@ -471,14 +375,114 @@
             t_copies[to][p][0].start()
         unpack_tail(slot, p)
 
-    for p in range(PARTS // 2):
-        take_part(p, 4, (3,))
-    for p in range(PARTS // 2):
+    def pass_ahead_part(p):
         for lanes in (1, 0):
             t_copies[3][p][lanes].wait_recv()
             for to in (2, 1, 0):
                 t_copies[to][p][lanes].start()
         unpack_tail(0, p)
+
+    def mask_lanes(block_step):
+        gi, ai = shifted(*block_step)
+        on = jnp.zeros((1, width), jnp.int32)
+        for j in range(7):
+            value = tm_ref[j, gi, ai] * exists(block_step, STEPS[j])
+            on = on + jnp.where(lane_block == j, value, 0)
+        return on.astype(F32)
+
+    own_lanes = mask_lanes(STEPS[0])
+    nothing = jnp.zeros((bs, bs), F32)
+
+    def place(slot, i, k, row_on, lanes_on, block):
+        pieces = []
+        for j in range(7):
+            k2 = second_step(i, j, k)
+            pieces.append(nothing if k2 is None else block(k2).astype(F32))
+        placed = jnp.concatenate(pieces, axis=1) * lanes_on * row_on
+        vs[slot, k * bs : (k + 1) * bs, :] = placed.astype(BF16)
+
+    def place_all(slot_steps):
+        lanes = [mask_lanes(STEPS[i]) for _, i in slot_steps]
+        for k in range(7):
+            row_on = (tm_ref[k, g, a] * exists(STEPS[k])).astype(F32)
+            for (slot, i), lanes_on in zip(slot_steps, lanes):
+                place(slot, i, k, row_on, lanes_on, lambda k2: block_of(vn[k], k2))
+
+    lax.fori_loop(8, 10, give_own, 0)
+    place_all([(0, 0), (1, 1), (2, 2)])
+    for parity in range(2):
+
+        @pl.when(odd == parity)
+        def _(parity=parity):
+            place_all([(3, BACK[towards(parity, 0)]), (4, BACK[towards(parity, 1)])])
+
+    take_part(0, 4, (3,))
+    lax.fori_loop(10, 12, give_own, 0)
+    def source_of(slot, zz, ww):
+        turn = slot >> 2
+        ahead = jnp.where(turn < half_line, half_line - turn, turn - (line - 1))
+        return (slot & (rows - 1)) * line + ((zz + ww * ahead + line) & (line - 1))
+
+    def spread(zz, ww):
+        down = lax.broadcasted_iota(jnp.int32, (tall, bs), 0) // slab
+        across = lax.broadcasted_iota(jnp.int32, (bs, tall), 1) // slab
+        tall_at = lax.broadcasted_iota(jnp.int32, (tall, bs), 1)
+        wide_at = lax.broadcasted_iota(jnp.int32, (bs, tall), 0)
+        as_rows = jnp.where(source_of(down, zz, ww) == tall_at, 1.0, 0.0).astype(BF16)
+        as_cols = jnp.where(source_of(across, zz, ww) == wide_at, 1.0, 0.0).astype(BF16)
+        return as_rows, as_cols
+
+    own_rows, own_cols = spread(z, way)
+    x_cols = spread(z, -way)[1]
+    z_rows, z_cols = spread(place_at(-1), way)
+
+    def weigh(slot, as_rows, block, as_cols):
+        stretched = jnp.dot(as_rows, block, preferred_element_type=F32).astype(BF16)
+        oexp[slot] = jnp.dot(stretched, as_cols, preferred_element_type=F32)
+
+    def by_way(up, down):
+        keep = odd.astype(F32)
+        both = block_of(occ, up).astype(F32) * (1.0 - keep) + block_of(occ, down).astype(F32) * keep
+        return both.astype(BF16)
+
+    weigh(0, own_rows, block_of(occ, 0), own_cols)
+    weigh(1, own_rows, block_of(occ, 1), x_cols)
+    weigh(2, own_rows, block_of(occ, 2), x_cols)
+    weigh(3, own_rows, by_way(3, 4), own_cols)
+    weigh(4, own_rows, by_way(5, 6), z_cols)
+
+    take_part(1, 4, (3,))
+    lax.fori_loop(12, 15, give_own, 0)
+    give(line - 1, z, z, rows - 1)
+    for axis in range(2):
+        p_copies[axis].wait_recv()
+    for parity in range(2):
+
+        @pl.when(odd == parity)
+        def _(parity=parity):
+            for axis in range(2):
+                i = towards(parity, axis)
+                ks = others(i)
+                source = STEPS[BACK[i]]
+                gs, a_s = shifted(*source)
+                for k in range(7):
+                    row_on = (tm_ref[k, gs, a_s] * exists(source, STEPS[k])).astype(F32)
+
+                    def block(k2, k=k):
+                        if k == 0:
+                            return block_of(vn[BACK[i]], k2)
+                        if k == i:
+                            return block_of(vn[0], k2)
+                        half = 0 if k2 == BACK[k] else 1
+                        return block_of(pack[2 + axis, ks.index(k)], half)
+
+                    place(5 + axis, i, k, row_on, own_lanes, block)
+                received = pack[2 + axis, ks.index(BACK[i])]
+                as_rows = own_rows if axis == 0 else z_rows
+                weigh(5 + axis, as_rows, block_of(received, 1), own_cols)
+
+    pass_ahead_part(0)
+    pass_ahead_part(1)
     for p in range(PARTS // 2, PARTS):
         take_part(p, 0, (3, 2, 1, 0))
 

time: 64.6 us -> 63.3 us (0.980)
  Pallas kernels: 63.2 us -> 61.9 us
    pallas_call x1, Pallas kernels: 63.2 us -> 61.9 us  [body(): pl.pallas_call(functools.partial(kernel, dims), out_shape=jax.ShapeDtypeS...]
where the time goes in v6:
time: 63.3 us; the launch traced here: 63.1 us
  Pallas kernels  61.9 us (98%)
  local copies, waits for them, and re-layouts  1.19 us (2%)
    pallas_call x1, Pallas kernels, body(): pl.pallas_call(functools.partial(kernel, dims), out_shape=jax.ShapeDtypeS...  61.9 us

profile of v6, /device:TPU:1, one launch (start us, length us, event | category | flops | bytes accessed | tf_op | source)
XLA Modules:
  0.0 63.1 jit_solution(4358129847652845733)
XLA Ops:
  0.0 61.9 %shard_map.73 = f32[1,8]{1,0:T(1,128)} custom-call(bf16[8,64,448]{2,1,0:T(8,128)(2,1)} %t_hbm.1, bf16[64,448]{1,0:T(8,128)(2,1)} %bitcast.5, bf16[64,448]{1,0:T(8,128)(2,1)} %bitcast.6, s32[7,8,64]{2,1,0:T(8,128)} %bitcast.7, s32[7,8,64]{2,1,0:T(8,128)} %bitcast.8, s32[7,8,64]{2,1,0:T(8,128)} %bitcast.9, s32[8,64]{1,0:T(8,128)} %sz_hbm.1), custom_call_target="tpu_custom_call" | custom-call | tf_op jit(solution)/shard_map/pallas_call | solution.py:598
  62.0 1.2 %copy.9 = f32[1,8]{1,0:T(1,128)} copy(f32[1,8]{1,0:T(1,128)} %shard_map.73) | data formatting | bytes 64

commit v7 on v6

--- a/solution.py
+++ b/solution.py
@@ -482,9 +482,9 @@
                 weigh(5 + axis, as_rows, block_of(received, 1), own_cols)
 
     pass_ahead_part(0)
+    take_part(2, 0, (3, 2, 1, 0))
     pass_ahead_part(1)
-    for p in range(PARTS // 2, PARTS):
-        take_part(p, 0, (3, 2, 1, 0))
+    take_part(3, 0, (3, 2, 1, 0))
 
     for s in range(5):
         xs[s] = jnp.dot(tn[0], vs[s], preferred_element_type=F32).astype(BF16)

time: 63.3 us -> 63.3 us (level)
  no operation moved by 1% of the time
where the time goes in v7:
time: 63.3 us; the launch traced here: 63.1 us
  Pallas kernels  61.9 us (98%)
  local copies, waits for them, and re-layouts  1.19 us (2%)
    pallas_call x1, Pallas kernels, body(): pl.pallas_call(functools.partial(kernel, dims), out_shape=jax.ShapeDtypeS...  61.9 us

profile of v7, /device:TPU:1, one launch (start us, length us, event | category | flops | bytes accessed | tf_op | source)
XLA Modules:
  0.0 63.1 jit_solution(3600051982125033965)
XLA Ops:
  0.0 61.9 %shard_map.73 = f32[1,8]{1,0:T(1,128)} custom-call(bf16[8,64,448]{2,1,0:T(8,128)(2,1)} %t_hbm.1, bf16[64,448]{1,0:T(8,128)(2,1)} %bitcast.5, bf16[64,448]{1,0:T(8,128)(2,1)} %bitcast.6, s32[7,8,64]{2,1,0:T(8,128)} %bitcast.7, s32[7,8,64]{2,1,0:T(8,128)} %bitcast.8, s32[7,8,64]{2,1,0:T(8,128)} %bitcast.9, s32[8,64]{1,0:T(8,128)} %sz_hbm.1), custom_call_target="tpu_custom_call" | custom-call | tf_op jit(solution)/shard_map/pallas_call | solution.py:598
  62.0 1.2 %copy.9 = f32[1,8]{1,0:T(1,128)} copy(f32[1,8]{1,0:T(1,128)} %shard_map.73) | data formatting | bytes 64
